TPU v7x, 128 devices: a whole 4x4x4 slice. The times are simulated.
128 devices in a mesh: north: 8 (over z, core), east: 16 (over y, x).
Axes of the slice: x: 4, y: 4, z: 4, core: 2. Of those that a mesh axis runs over, the one named last changes fastest.
Arguments:
- gates: bfloat16 [32768, 16, 128], P(('north', 'east')), may hold values from -6 to 6
- mixing_weight_blocks: bfloat16 [32768, 128, 128], P(('north', 'east')), may hold values from -0.5 to 0.5
- send_pick: int32 [128, 128, 2], P(('north', 'east')), may hold values from -1 to 255, as said below
- feed: int32 [128, 256], P(('north', 'east')), may hold values from -1 to 255, as said below
- window: int32 [128, 256], P(('north', 'east')), may hold values from 0 to 127, as said below
- proj_weight: bfloat16 [64, 64], replicated, may hold values from -0.75 to 0.75
- conv_weight: bfloat16 [3, 9, 64, 64], replicated, may hold values from -0.25 to 0.25
- rates: int32 [3], replicated, may hold values from 1 to 4, as said below
Outputs:
- nowcast_features: bfloat16 [64, 256, 2048], P(None, 'north', 'east')
Inputs may be any that keep to these rules, and one draw needn't show every extreme that they name: `send_pick`: -1 marks an empty slot; other entries are the source device's own sweep blocks, distinct within one source and destination, filled slots first; some source fills all 2 slots to some owner. `feed`: -1 marks padding; every filled slot sent to an owner is named exactly once in its list and no empty slot is named; used entries come first, at least 128 of them in every list; some owner has all 256 entries used. Every window of every owner's tile is named by at least one used entry of that owner's list. `rates`: some layer has rate 4.
All inputs are finite; a program needn't handle non-finite values.
Results may differ from a plain program's by a relative error of at most 0.0063.
Values may be sent and summed in bfloat16 or wider, within the bound.
A program may use at most 128 MiB of HBM per device.

v0:
```python
import functools

import jax
import jax.numpy as jnp
from jax import lax
from jax.experimental import pallas as pl
from jax.experimental.pallas import tpu as pltpu
from jax.sharding import PartitionSpec as P

MESH = pl.DeviceIdType.MESH
NN, NE = 8, 16
ND = NN * NE
GATES = 128
FEATS = 16
CHANNELS = 64
LAYERS = 3
HALO = 4
HR, HC = 32, 128
PMAX = 256
BF, F32 = jnp.bfloat16, jnp.float32


def exchange_kernel(pick, gates, out, s0, s1, m0, m1, ssem, rsem):
    n, e = lax.axis_index("north"), lax.axis_index("east")
    bar = pltpu.get_barrier_semaphore()
    peers_e = [lax.rem(e + i, NE) for i in range(1, NE)]
    peers_n = [lax.rem(n + i, NN) for i in range(1, NN)]
    for te in peers_e:
        pl.semaphore_signal(bar, inc=1, device_id=(n, te), device_id_type=MESH)
    for tn in peers_n:
        pl.semaphore_signal(bar, inc=1, device_id=(tn, e), device_id_type=MESH)

    def gather(t, carry):
        tn, te = t // NE, lax.rem(t, NE)
        for k in range(2):
            p = pick[0, 2 * t + k]
            v = gates[jnp.maximum(p, 0)]
            v = jnp.where(p >= 0, v, jnp.zeros_like(v))
            if k == 0:
                s0[te, tn] = v
            else:
                s1[tn, te] = v
        return carry

    lax.fori_loop(0, ND, gather, 0, unroll=8)
    pl.semaphore_wait(bar, NE + NN - 2)
    f0, f1 = out.at[0], out.at[1]

    def remote(src, dst, k, dev):
        return pltpu.make_async_remote_copy(
            src_ref=src, dst_ref=dst, send_sem=ssem.at[k], recv_sem=rsem.at[k],
            device_id=dev, device_id_type=MESH,
        )

    for i in range(NE - 1):
        remote(s0.at[peers_e[i]], m0.at[e], 0, (n, peers_e[i])).start()
        if i < NN - 1:
            remote(s1.at[peers_n[i]], m1.at[n], 1, (peers_n[i], e)).start()
    m0[e] = s0[e]
    m1[n] = s1[n]

    def wait(ref, count, sem):
        r = ref.at[pl.ds(0, count)]
        pltpu.make_async_copy(r, r, sem).wait()

    wait(m1, NN - 1, rsem.at[1])
    for te in peers_e:
        remote(m1.at[:, te], f1.at[pl.ds(e * NN, NN)], 3, (n, te)).start()
    f1[pl.ds(e * NN, NN)] = m1[:, e]
    wait(m0, NE - 1, rsem.at[0])
    for tn in peers_n:
        remote(m0.at[:, tn], f0.at[pl.ds(n * NE, NE)], 2, (tn, e)).start()
    f0[pl.ds(n * NE, NE)] = m0[:, n]
    wait(f1, ND - NN, rsem.at[3])
    wait(f0, ND - NE, rsem.at[2])
    wait(m0, NE - 1, ssem.at[0])
    wait(m1, NN - 1, ssem.at[1])
    wait(f0, ND - NE, ssem.at[2])
    wait(f1, ND - NN, ssem.at[3])


def exchange(pick, gates):
    blk = (FEATS, GATES)
    return pl.pallas_call(
        exchange_kernel,
        out_shape=jax.ShapeDtypeStruct((2, ND) + blk, BF),
        in_specs=[pl.BlockSpec(memory_space=pltpu.SMEM), pl.BlockSpec(memory_space=pltpu.VMEM)],
        out_specs=pl.BlockSpec(memory_space=pltpu.VMEM),
        scratch_shapes=[
            pltpu.VMEM((NE, NN) + blk, BF), pltpu.VMEM((NN, NE) + blk, BF),
            pltpu.VMEM((NE, NN) + blk, BF), pltpu.VMEM((NN, NE) + blk, BF),
            pltpu.SemaphoreType.DMA((4,)), pltpu.SemaphoreType.DMA((4,)),
        ],
        compiler_params=pltpu.CompilerParams(
            collective_id=0, has_side_effects=True, vmem_limit_bytes=40 << 20),
        name="exchange",
    )(pick, gates)


NCH = 8
CH = PMAX // NCH


def iota(shape, dim):
    return lax.broadcasted_iota(jnp.int32, shape, dim)


def blend_kernel(feed_s, feed_v, win_v, rows, w_hbm, proj, x0, wbuf, share, grid, sem):
    for c in range(NCH):
        pltpu.make_async_copy(w_hbm.at[pl.ds(c * CH, CH)], wbuf.at[pl.ds(c * CH, CH)], sem.at[c]).start()
    hot = (win_v[...] == iota((GATES, PMAX), 0)) & (feed_v[...] >= 0)
    hot = jnp.where(hot, 1.0, 0.0).astype(BF)
    hot2 = jnp.concatenate([hot, hot], axis=1)

    def product(p, carry):
        j = jnp.maximum(feed_s[0, p], 0)
        s, k = j // 2, lax.rem(j, 2)
        q = jnp.where(k == 0, s, lax.rem(s, NE) * NN + s // NE)
        share[pl.ds(pl.multiple_of(p * FEATS, FEATS), FEATS), :] = jnp.dot(
            rows[k, q], wbuf[p], preferred_element_type=F32)
        return carry

    for c in range(NCH):
        pltpu.make_async_copy(w_hbm.at[pl.ds(c * CH, CH)], wbuf.at[pl.ds(c * CH, CH)], sem.at[c]).wait()
        lax.fori_loop(c * CH, c * CH + CH, product, 0, unroll=16)
    for f in range(0, FEATS, 2):
        parts = []
        for g in (f, f + 1):
            v = share[pl.ds(g, PMAX, stride=FEATS), :]
            hi = v.astype(BF)
            lo = (v - hi.astype(F32)).astype(BF)
            parts.append(jnp.concatenate([hi, lo], axis=0))
        r = jnp.dot(hot2, jnp.concatenate(parts, axis=1), preferred_element_type=F32)
        grid[pl.ds(f, 128, stride=FEATS), :] = r[:, :128]
        grid[pl.ds(f + 1, 128, stride=FEATS), :] = r[:, 128:]

    col = iota((1, 512), 1)
    i1, w1, a1, b1, j1 = col // 128, col // 32 % 4, col // 16 % 2, col // 8 % 2, col % 8
    src1 = w1 * 128 + i1 * 32 + a1 * 16 + j1 * 2 + b1
    t1 = jnp.where(iota((512, 512), 0) == src1, 1.0, 0.0).astype(BF)
    q2, wh2, wl2, j2 = col // 128, col // 32 % 4, col // 8 % 4, col % 8
    src2 = wh2 * 128 + wl2 * 32 + q2 * 8 + j2
    t2 = jnp.where(iota((512, 512), 0) == src2, 1.0, 0.0).astype(BF)
    tiles = []
    for wh in range(4):
        line = []
        for wl in range(4):
            wc = wh * 4 + wl
            blocks = [grid[pl.ds((wr * 16 + wc) * FEATS, FEATS), :] for wr in range(8)]
            line.append(jnp.concatenate(blocks, axis=0).astype(BF))
        tiles.append(jnp.concatenate(line, axis=1))
    y = jnp.dot(jnp.concatenate(tiles, axis=0), t1, preferred_element_type=F32).astype(BF)
    tiles = [
        jnp.concatenate([y[wh * 128:(wh + 1) * 128, i * 128:(i + 1) * 128] for wh in range(4)], axis=1)
        for i in range(4)
    ]
    z = jnp.dot(jnp.concatenate(tiles, axis=0), t2, preferred_element_type=F32).astype(BF)
    for wr in range(8):
        cells = []
        for i in range(4):
            r0 = (i * 8 + wr) * FEATS
            cells.append(jnp.concatenate(
                [z[r0:r0 + FEATS, q * 128:(q + 1) * 128] for q in range(4)], axis=0))
        o = jnp.dot(proj[...], jnp.concatenate(cells, axis=1), preferred_element_type=F32)
        o = jax.nn.gelu(o).astype(BF)
        for i in range(4):
            x0[wr * 4 + i] = o[:, i * 128:(i + 1) * 128]


def blend(feed, window, rows, w, proj):
    vm = pl.BlockSpec(memory_space=pltpu.VMEM)
    return pl.pallas_call(
        blend_kernel,
        out_shape=jax.ShapeDtypeStruct((HR, CHANNELS, HC), BF),
        in_specs=[pl.BlockSpec(memory_space=pltpu.SMEM), vm, vm, vm, pl.BlockSpec(memory_space=pl.ANY), vm],
        out_specs=vm,
        scratch_shapes=[
            pltpu.VMEM((PMAX, GATES, 128), BF),
            pltpu.VMEM((PMAX * FEATS, 128), F32),
            pltpu.VMEM((128 * FEATS, 128), F32),
            pltpu.SemaphoreType.DMA((NCH,)),
        ],
        compiler_params=pltpu.CompilerParams(vmem_limit_bytes=40 << 20),
        name="blend",
    )(feed, feed, window, rows, w, proj)


ER = HR + 2 * HALO


def conv_kernel(rates, x0, wall, out, ext, edges, halo, ybuf, fbuf, ssem, rsem):
    n, e = lax.axis_index("north"), lax.axis_index("east")
    up, down = lax.rem(n + NN - 1, NN), lax.rem(n + 1, NN)
    left, right = lax.rem(e + NE - 1, NE), lax.rem(e + 1, NE)
    bar = pltpu.get_barrier_semaphore()
    for tn in (up, n, down):
        for te in (left, e, right):
            if tn is n and te is e:
                continue
            pl.semaphore_signal(bar, inc=1, device_id=(tn, te), device_id_type=MESH)
    lane = iota((CHANNELS, HC), 1)
    row_ok = [(n > 0), None, (n < NN - 1)]
    col_ok = [(e > 0), (e < NE - 1)]

    def pack(layer, get):
        el = jnp.zeros((CHANNELS, HC), F32)
        er = jnp.zeros((CHANNELS, HC), F32)
        for r in range(HR):
            v = get(r)
            here = (lane // HALO) == r
            el = jnp.where(here, pltpu.roll(v, 4 * r, 1) if r else v, el)
            er = jnp.where(here, pltpu.roll(v, (4 * r + 4) % 128, 1) if r < HR - 1 else v, er)
        edges[layer, 0] = el.astype(BF)
        edges[layer, 1] = er.astype(BF)

    def load(i, carry):
        ext[0, i + HALO] = x0[i]
        fbuf[pl.ds(pl.multiple_of(i * CHANNELS, CHANNELS), CHANNELS), :] = x0[i].astype(F32)
        return carry

    lax.fori_loop(0, HR, load, 0, unroll=8)

    for layer in range(LAYERS):
        pack(layer, lambda r: fbuf[r * CHANNELS:(r + 1) * CHANNELS, :])
        if layer == 0:
            pl.semaphore_wait(bar, 8)

        def remote(src, dst, dev):
            cp = pltpu.make_async_remote_copy(
                src_ref=src, dst_ref=dst, send_sem=ssem.at[layer], recv_sem=rsem.at[layer],
                device_id=dev, device_id_type=MESH)
            cp.start()

        remote(ext.at[layer, pl.ds(HALO, HALO)], ext.at[layer, pl.ds(HALO + HR, HALO)], (up, e))
        remote(ext.at[layer, pl.ds(HR, HALO)], ext.at[layer, pl.ds(0, HALO)], (down, e))
        for k, tn in ((2, up), (1, n), (0, down)):
            remote(edges.at[layer, 1], halo.at[layer, k], (tn, right))
            remote(edges.at[layer, 0], halo.at[layer, 3 + k], (tn, left))
        everything = ext.at[layer, pl.ds(0, 14)]
        pltpu.make_async_copy(everything, everything, rsem.at[layer]).wait()

        d = rates[layer]
        w = wall[layer]

        def one_row(m, k, rr):
            x = ext[layer, m].astype(F32)
            lt = halo[layer, k].astype(F32)
            rt = halo[layer, 3 + k].astype(F32)
            ok = row_ok[k]
            if ok is not None:
                x = jnp.where(ok, x, 0.0)
            okl = col_ok[0] if ok is None else jnp.logical_and(ok, col_ok[0])
            okr = col_ok[1] if ok is None else jnp.logical_and(ok, col_ok[1])
            lt = jnp.where(okl, lt, 0.0)
            rt = jnp.where(okr, rt, 0.0)
            lt = pltpu.roll(lt, lax.rem(d + 124 - 4 * rr + 128, 128), 1)
            xl = jnp.where(lane >= d, pltpu.roll(x, d, 1), lt)
            rt = pltpu.roll(rt, lax.rem(256 - d - 4 * rr, 128), 1)
            xr = jnp.where(lane < HC - d, pltpu.roll(x, HC - d, 1), rt)
            return jnp.concatenate([xl.astype(BF), x.astype(BF), xr.astype(BF)], axis=0)

        def two_rows(m, k, rr):
            b = jnp.concatenate([one_row(m, k, rr), one_row(m + 1, k, rr + 1)], axis=1)
            y = jnp.dot(w, b, preferred_element_type=F32)
            ybuf[m] = y[:, :HC]
            ybuf[m + 1] = y[:, HC:]

        for m in (0, 2):
            two_rows(m, 0, HR - HALO + m)
        lax.fori_loop(0, HR // 2, lambda i, c: (two_rows(HALO + 2 * i, 1, 2 * i), c)[1], 0, unroll=4)
        for m in (0, 2):
            two_rows(HALO + HR + m, 2, m)

        def finish(i, carry):
            h = (ybuf[i + HALO - d, 0:64, :] + ybuf[i + HALO, 64:128, :]
                 + ybuf[i + HALO + d, 128:192, :])
            at = pl.ds(pl.multiple_of(i * CHANNELS, CHANNELS), CHANNELS)
            v = (fbuf[at, :] + jax.nn.gelu(h)).astype(BF)
            fbuf[at, :] = v.astype(F32)
            if layer < LAYERS - 1:
                ext[layer + 1, i + HALO] = v
            return carry

        lax.fori_loop(0, HR, finish, 0, unroll=4)

    for c in range(CHANNELS):
        out[c] = fbuf[pl.ds(c, HR, stride=CHANNELS), :].astype(BF)
    for layer in range(LAYERS):
        everything = ext.at[layer, pl.ds(0, 14)]
        pltpu.make_async_copy(everything, everything, ssem.at[layer]).wait()


def conv(rates, x0, wall):
    vm = pl.BlockSpec(memory_space=pltpu.VMEM)
    return pl.pallas_call(
        conv_kernel,
        out_shape=jax.ShapeDtypeStruct((CHANNELS, HR, HC), BF),
        in_specs=[pl.BlockSpec(memory_space=pltpu.SMEM), vm, vm],
        out_specs=vm,
        scratch_shapes=[
            pltpu.VMEM((LAYERS, ER, CHANNELS, HC), BF),
            pltpu.VMEM((LAYERS, 2, CHANNELS, HC), BF),
            pltpu.VMEM((LAYERS, 6, CHANNELS, HC), BF),
            pltpu.VMEM((ER, 3 * CHANNELS, HC), F32),
            pltpu.VMEM((HR * CHANNELS, HC), F32),
            pltpu.SemaphoreType.DMA((LAYERS,)), pltpu.SemaphoreType.DMA((LAYERS,)),
        ],
        compiler_params=pltpu.CompilerParams(
            collective_id=1, has_side_effects=True, vmem_limit_bytes=40 << 20),
        name="conv",
    )(rates, x0, wall)


def per_device(gates, mixing_weight_blocks, send_pick, feed, window, proj_weight, conv_weight, rates):
    rows = exchange(send_pick.reshape(1, 2 * ND), gates)
    proj = proj_weight.reshape(CHANNELS, FEATS, 4).transpose(0, 2, 1).reshape(CHANNELS, 4 * FEATS)
    x0 = blend(feed, window, rows, mixing_weight_blocks, proj)
    wall = conv_weight.reshape(LAYERS, 3, 3, CHANNELS, CHANNELS).transpose(0, 1, 3, 2, 4)
    wall = wall.reshape(LAYERS, 3 * CHANNELS, 3 * CHANNELS)
    return conv(rates, x0, wall)


def solution(mesh):
    in_specs = (
        P(("north", "east"), None, None),
        P(("north", "east"), None, None),
        P(("north", "east"), None, None),
        P(("north", "east"), None),
        P(("north", "east"), None),
        P(),
        P(),
        P(),
    )
    return jax.shard_map(
        per_device, mesh=mesh, in_specs=in_specs, out_specs=P(None, "north", "east"), check_vma=False
    )
```

profile of v0, /device:TPU:1, one launch (start us, length us, event | category | flops | bytes accessed | tf_op | source)
XLA Modules:
  0.0 71.8 jit_solution(6939555216579702760)
XLA Ops:
  0.0 0.0 copy-start.4
  0.0 0.8 %copy.12 = s32[1,128,2]{2,1,0:T(8,128)S(1)} copy(s32[1,128,2]{1,2,0:T(2,128)} %param.10) | data formatting | bytes 2048 | tf_op args[2]
  0.8 0.1 reshape.15.pick
  0.9 0.0 copy-start.1
  1.0 1.2 %copy-done.1 = bf16[256,16,128]{2,1,0:T(8,128)(2,1)S(1)} copy-done((bf16[256,16,128]{2,1,0:T(8,128)(2,1)S(1)}, bf16[256,16,128]{2,1,0:T(8,128)(2,1)}, u32[]{:S(2)}) %copy-start.1) | copy-done | bytes 1048600
  2.2 0.0 copy-start.5
  2.2 25.7 %exchange.1.rows = bf16[2,128,16,128]{3,2,1,0:T(8,128)(2,1)S(1)} custom-call(s32[1,256]{1,0:T(1,128)S(1)} %reshape.15.pick, bf16[256,16,128]{2,1,0:T(8,128)(2,1)S(1)} %copy-done.1), custom_call_target="tpu_custom_call" | custom-call | tf_op jit(solution)/shard_map/exchange/pallas_call | solution.py:84
  27.9 0.8 %copy.13 = bf16[64,64]{0,1:T(8,128)(2,1)S(1)} copy(bf16[64,64]{1,0:T(8,128)(2,1)} %param.13) | data formatting | bytes 16384 | tf_op args[5]
  28.7 0.1 copy.15.proj
  28.8 0.0 copy-start
  28.8 3.4 %copy-done = bf16[256,128,128]{2,1,0:T(8,128)(2,1)S(1)} copy-done((bf16[256,128,128]{2,1,0:T(8,128)(2,1)S(1)}, bf16[256,128,128]{2,1,0:T(8,128)(2,1)}, u32[]{:S(2)}) %copy-start) | copy-done | bytes 8388632
  32.2 0.0 copy-start.2
  32.2 0.7 copy-done.2
  32.9 0.0 copy-start.3
  32.9 0.7 copy-done.3
  33.5 8.0 %blend.1.x0 = bf16[32,64,128]{2,1,0:T(8,128)(2,1)S(1)} custom-call(s32[1,256]{1,0:T(1,128)S(1)} %copy-done.2, s32[1,256]{1,0:T(1,128)S(1)} %copy-done.2, s32[1,256]{1,0:T(1,128)S(1)} %copy-done.3, bf16[2,128,16,128]{3,2,1,0:T(8,128)(2,1)S(1)} %exchange.1.rows, bf16[256,128,128]{2,1,0:T(8,128)(2,1)S(1)} %copy-done, bf16[64,64]{1,0:T(8,128)(2,1)S(1)} %copy.15.proj), custom_call_target="tpu_custom_call" | custom-call | tf_op jit(solution)/shard_map/blend/pallas_call | solution.py:172
  41.6 0.0 copy-done.5
  41.6 0.4 copy.18
  42.0 0.4 reshape.19.wall
  42.3 0.0 copy-done.4
  42.3 28.6 %conv.1 = bf16[64,32,128]{2,1,0:T(8,128)(2,1)S(1)} custom-call(s32[3]{0:T(128)S(1)} %copy-done.4, bf16[32,64,128]{2,1,0:T(8,128)(2,1)S(1)} %blend.1.x0, bf16[3,192,192]{2,1,0:T(8,128)(2,1)S(1)} %reshape.19.wall), custom_call_target="tpu_custom_call" | custom-call | tf_op jit(solution)/shard_map/conv/pallas_call | solution.py:295
  71.0 0.8 %copy.20 = bf16[64,32,128]{2,1,0:T(8,128)(2,1)} copy(bf16[64,32,128]{2,1,0:T(8,128)(2,1)S(1)} %conv.1) | data formatting | bytes 1048576
  (1 shorter events, 0.0 us)
Async XLA Ops:
  0.0 42.3 %copy-start.4 = (s32[3]{0:T(128)S(1)}, s32[3]{0:T(128)}, u32[]{:S(2)}) copy-start(s32[3]{0:T(128)} %rates.1) | copy-start | bytes 40
  0.9 1.2 %copy-start.1 = (bf16[256,16,128]{2,1,0:T(8,128)(2,1)S(1)}, bf16[256,16,128]{2,1,0:T(8,128)(2,1)}, u32[]{:S(2)}) copy-start(bf16[256,16,128]{2,1,0:T(8,128)(2,1)} %gates.1) | copy-start | bytes 3145732
  2.2 39.4 %copy-start.5 = (bf16[3,9,64,64]{3,2,1,0:T(8,128)(2,1)S(1)}, bf16[3,9,64,64]{3,2,1,0:T(8,128)(2,1)}, u32[]{:S(2)}) copy-start(bf16[3,9,64,64]{3,2,1,0:T(8,128)(2,1)} %param.14) | copy-start | bytes 663556
  28.8 3.4 %copy-start = (bf16[256,128,128]{2,1,0:T(8,128)(2,1)S(1)}, bf16[256,128,128]{2,1,0:T(8,128)(2,1)}, u32[]{:S(2)}) copy-start(bf16[256,128,128]{2,1,0:T(8,128)(2,1)} %w_hbm.1) | copy-start | bytes 25165828
  32.2 0.7 copy-start.2
  32.9 0.7 copy-start.3
where the time goes:
time: 72.3 us; the launch traced here: 71.8 us
  Pallas kernels  62.4 us (86%)
  local copies, waits for them, and re-layouts  9.34 us (13%)
    pallas_call x1, Pallas kernels, conv(): pl.pallas_call(conv_kernel, out_shape=jax.ShapeDtypeStruct((CHANNELS, HR,...  28.6 us
    pallas_call x1, Pallas kernels, exchange(): pl.pallas_call(exchange_kernel, out_shape=jax.ShapeDtypeStruct((2, ND) +...  25.7 us
    unnamed x15, local copies, waits for them, and re-layouts  8.37 us
    pallas_call x1, Pallas kernels, blend(): pl.pallas_call(blend_kernel, out_shape=jax.ShapeDtypeStruct((HR, CHANNELS...  8.04 us

commit v1 on v0

v1 whole, which is shorter than its diff:
```python
import functools

import jax
import jax.numpy as jnp
from jax import lax
from jax.experimental import pallas as pl
from jax.experimental.pallas import tpu as pltpu
from jax.sharding import PartitionSpec as P

MESH = pl.DeviceIdType.MESH
NN, NE = 8, 16
ND = NN * NE
GATES = 128
FEATS = 16
CHANNELS = 64
LAYERS = 3
HALO = 4
HR, HC = 32, 128
PMAX = 256
BF, F32 = jnp.bfloat16, jnp.float32


NCH = 8
CH = PMAX // NCH
ER = HR + 2 * HALO


def iota(shape, dim):
    return lax.broadcasted_iota(jnp.int32, shape, dim)


def places():
    n, e = lax.axis_index("north"), lax.axis_index("east")
    up, down = lax.rem(n + NN - 1, NN), lax.rem(n + 1, NN)
    left, right = lax.rem(e + NE - 1, NE), lax.rem(e + 1, NE)
    return n, e, up, down, left, right


def exchange(pick, gates, s0, s1, m0, m1, rows, ssem, rsem, bar, meanwhile):
    n, e, up, down, left, right = places()
    peers_e = [lax.rem(e + i, NE) for i in range(1, NE)]
    peers_n = [lax.rem(n + i, NN) for i in range(1, NN)]

    def gather(t, carry):
        tn, te = t // NE, lax.rem(t, NE)
        for k in range(2):
            p = pick[0, k, t]
            v = gates[jnp.maximum(p, 0)]
            v = jnp.where(p >= 0, v, jnp.zeros_like(v))
            if k == 0:
                s0[te, tn] = v
            else:
                s1[tn, te] = v
        return carry

    lax.fori_loop(0, ND, gather, 0, unroll=8)
    pl.semaphore_wait(bar, NE + NN - 2 + 4)
    f0, f1 = rows.at[0], rows.at[1]

    def remote(src, dst, k, dev):
        return pltpu.make_async_remote_copy(
            src_ref=src, dst_ref=dst, send_sem=ssem.at[k], recv_sem=rsem.at[k],
            device_id=dev, device_id_type=MESH,
        )

    for i in range(NE - 1):
        remote(s0.at[peers_e[i]], m0.at[e], 0, (n, peers_e[i])).start()
        if i < NN - 1:
            remote(s1.at[peers_n[i]], m1.at[n], 1, (peers_n[i], e)).start()
    m0[e] = s0[e]
    m1[n] = s1[n]
    meanwhile()

    def wait(ref, count, sem):
        r = ref.at[pl.ds(0, count)]
        pltpu.make_async_copy(r, r, sem).wait()

    wait(m1, NN - 1, rsem.at[1])
    for te in peers_e:
        remote(m1.at[:, te], f1.at[pl.ds(e * NN, NN)], 3, (n, te)).start()
    f1[pl.ds(e * NN, NN)] = m1[:, e]
    wait(m0, NE - 1, rsem.at[0])
    for tn in peers_n:
        remote(m0.at[:, tn], f0.at[pl.ds(n * NE, NE)], 2, (tn, e)).start()
    f0[pl.ds(n * NE, NE)] = m0[:, n]
    wait(f1, ND - NN, rsem.at[3])
    wait(f0, ND - NE, rsem.at[2])

    def sent():
        wait(m0, NE - 1, ssem.at[0])
        wait(m1, NN - 1, ssem.at[1])
        wait(f0, ND - NE, ssem.at[2])
        wait(f1, ND - NN, ssem.at[3])

    return sent


def tables(win_v, feed_v, proj, taps, hot2, t1, t2, projq, wall):
    hot = (win_v[...] == iota((GATES, PMAX), 0)) & (feed_v[...] >= 0)
    hot = jnp.where(hot, 1.0, 0.0).astype(BF)
    hot2[...] = jnp.concatenate([hot, hot], axis=1)
    col = iota((1, 512), 1)
    i1, w1, a1, b1, j1 = col // 128, col // 32 % 4, col // 16 % 2, col // 8 % 2, col % 8
    src1 = w1 * 128 + i1 * 32 + a1 * 16 + j1 * 2 + b1
    t1[...] = jnp.where(iota((512, 512), 0) == src1, 1.0, 0.0).astype(BF)
    q2, wh2, wl2, j2 = col // 128, col // 32 % 4, col // 8 % 4, col % 8
    src2 = wh2 * 128 + wl2 * 32 + q2 * 8 + j2
    t2[...] = jnp.where(iota((512, 512), 0) == src2, 1.0, 0.0).astype(BF)
    c = iota((1, 64), 1)
    p = jnp.where(iota((64, 64), 0) == c % 16 * 4 + c // 16, 1.0, 0.0).astype(BF)
    projq[...] = jnp.dot(proj[...], p, preferred_element_type=F32).astype(BF)
    for layer in range(LAYERS):
        for a in range(3):
            line = [taps[layer, a * 3 + b].astype(F32) for b in range(3)]
            wall[layer, a * CHANNELS:(a + 1) * CHANNELS, :] = jnp.concatenate(line, axis=1).astype(BF)


def blend(feed_s, rows, wbuf, share, grid, hot2, t1, t2, projq, wait_w, put):
    def product(p, carry):
        j = jnp.maximum(feed_s[0, p], 0)
        s, k = j // 2, lax.rem(j, 2)
        q = jnp.where(k == 0, s, lax.rem(s, NE) * NN + s // NE)
        share[pl.ds(pl.multiple_of(p * FEATS, FEATS), FEATS), :] = jnp.dot(
            rows[k, q], wbuf[p], preferred_element_type=F32)
        return carry

    wait_w()
    lax.fori_loop(0, PMAX, product, 0, unroll=16)
    for f in range(0, FEATS, 2):
        parts = []
        for g in (f, f + 1):
            v = share[pl.ds(g, PMAX, stride=FEATS), :]
            hi = v.astype(BF)
            lo = (v - hi.astype(F32)).astype(BF)
            parts.append(jnp.concatenate([hi, lo], axis=0))
        r = jnp.dot(hot2[...], jnp.concatenate(parts, axis=1), preferred_element_type=F32)
        grid[pl.ds(f, 128, stride=FEATS), :] = r[:, :128]
        grid[pl.ds(f + 1, 128, stride=FEATS), :] = r[:, 128:]

    tiles = []
    for wh in range(4):
        line = []
        for wl in range(4):
            wc = wh * 4 + wl
            blocks = [grid[pl.ds((wr * 16 + wc) * FEATS, FEATS), :] for wr in range(8)]
            line.append(jnp.concatenate(blocks, axis=0).astype(BF))
        tiles.append(jnp.concatenate(line, axis=1))
    y = jnp.dot(jnp.concatenate(tiles, axis=0), t1[...], preferred_element_type=F32).astype(BF)
    tiles = [
        jnp.concatenate([y[wh * 128:(wh + 1) * 128, i * 128:(i + 1) * 128] for wh in range(4)], axis=1)
        for i in range(4)
    ]
    z = jnp.dot(jnp.concatenate(tiles, axis=0), t2[...], preferred_element_type=F32).astype(BF)
    for wr in range(8):
        cells = []
        for i in range(4):
            r0 = (i * 8 + wr) * FEATS
            cells.append(jnp.concatenate(
                [z[r0:r0 + FEATS, q * 128:(q + 1) * 128] for q in range(4)], axis=0))
        o = jnp.dot(projq[...], jnp.concatenate(cells, axis=1), preferred_element_type=F32)
        o = jax.nn.gelu(o).astype(BF)
        for i in range(4):
            put(wr * 4 + i, o[:, i * 128:(i + 1) * 128])


def conv(rates, wall, out, ext, edges, halo, ybuf, fbuf, ssem, rsem):
    n, e, up, down, left, right = places()
    lane = iota((CHANNELS, HC), 1)
    row_ok = [(n > 0), None, (n < NN - 1)]
    col_ok = [(e > 0), (e < NE - 1)]

    def pack(layer, get):
        el = jnp.zeros((CHANNELS, HC), F32)
        er = jnp.zeros((CHANNELS, HC), F32)
        for r in range(HR):
            v = get(r)
            here = (lane // HALO) == r
            el = jnp.where(here, pltpu.roll(v, 4 * r, 1) if r else v, el)
            er = jnp.where(here, pltpu.roll(v, (4 * r + 4) % 128, 1) if r < HR - 1 else v, er)
        edges[layer, 0] = el.astype(BF)
        edges[layer, 1] = er.astype(BF)

    for layer in range(LAYERS):
        pack(layer, lambda r: fbuf[r * CHANNELS:(r + 1) * CHANNELS, :])

        def remote(src, dst, dev):
            cp = pltpu.make_async_remote_copy(
                src_ref=src, dst_ref=dst, send_sem=ssem.at[layer], recv_sem=rsem.at[layer],
                device_id=dev, device_id_type=MESH)
            cp.start()

        remote(ext.at[layer, pl.ds(HALO, HALO)], ext.at[layer, pl.ds(HALO + HR, HALO)], (up, e))
        remote(ext.at[layer, pl.ds(HR, HALO)], ext.at[layer, pl.ds(0, HALO)], (down, e))
        for k, tn in ((2, up), (1, n), (0, down)):
            remote(edges.at[layer, 1], halo.at[layer, k], (tn, right))
            remote(edges.at[layer, 0], halo.at[layer, 3 + k], (tn, left))
        everything = ext.at[layer, pl.ds(0, 14)]
        pltpu.make_async_copy(everything, everything, rsem.at[layer]).wait()

        d = rates[layer]
        w = wall[layer]

        def one_row(m, k, rr):
            x = ext[layer, m].astype(F32)
            lt = halo[layer, k].astype(F32)
            rt = halo[layer, 3 + k].astype(F32)
            ok = row_ok[k]
            if ok is not None:
                x = jnp.where(ok, x, 0.0)
            okl = col_ok[0] if ok is None else jnp.logical_and(ok, col_ok[0])
            okr = col_ok[1] if ok is None else jnp.logical_and(ok, col_ok[1])
            lt = jnp.where(okl, lt, 0.0)
            rt = jnp.where(okr, rt, 0.0)
            lt = pltpu.roll(lt, lax.rem(d + 124 - 4 * rr + 128, 128), 1)
            xl = jnp.where(lane >= d, pltpu.roll(x, d, 1), lt)
            rt = pltpu.roll(rt, lax.rem(256 - d - 4 * rr, 128), 1)
            xr = jnp.where(lane < HC - d, pltpu.roll(x, HC - d, 1), rt)
            return jnp.concatenate([xl.astype(BF), x.astype(BF), xr.astype(BF)], axis=0)

        def two_rows(m, k, rr):
            b = jnp.concatenate([one_row(m, k, rr), one_row(m + 1, k, rr + 1)], axis=1)
            y = jnp.dot(w, b, preferred_element_type=F32)
            ybuf[m] = y[:, :HC]
            ybuf[m + 1] = y[:, HC:]

        for m in (0, 2):
            two_rows(m, 0, HR - HALO + m)
        lax.fori_loop(0, HR // 2, lambda i, c: (two_rows(HALO + 2 * i, 1, 2 * i), c)[1], 0, unroll=4)
        for m in (0, 2):
            two_rows(HALO + HR + m, 2, m)

        def finish(i, carry):
            h = (ybuf[i + HALO - d, 0:64, :] + ybuf[i + HALO, 64:128, :]
                 + ybuf[i + HALO + d, 128:192, :])
            at = pl.ds(pl.multiple_of(i * CHANNELS, CHANNELS), CHANNELS)
            v = (fbuf[at, :] + jax.nn.gelu(h)).astype(BF)
            fbuf[at, :] = v.astype(F32)
            if layer < LAYERS - 1:
                ext[layer + 1, i + HALO] = v
            return carry

        lax.fori_loop(0, HR, finish, 0, unroll=4)

    for c in range(CHANNELS):
        out[c] = fbuf[pl.ds(c, HR, stride=CHANNELS), :].astype(BF)
    for layer in range(LAYERS):
        everything = ext.at[layer, pl.ds(0, 14)]
        pltpu.make_async_copy(everything, everything, ssem.at[layer]).wait()


def kernel(pick, feed_s, rates, feed_v, win_v, gates_hbm, w_hbm, proj, taps, out,
           s0, s1, m0, m1, rows, gates, wbuf, share, grid, hot2, t1, t2, projq, wall,
           ext, edges, halo, ybuf, fbuf, asem, arem, ssem, rsem, lsem):
    n, e, up, down, left, right = places()
    load_g = pltpu.make_async_copy(gates_hbm, gates, lsem.at[0])
    load_g.start()
    load_w = pltpu.make_async_copy(w_hbm, wbuf, lsem.at[1])
    load_w.start()
    bar = pltpu.get_barrier_semaphore()
    for i in range(1, NE):
        pl.semaphore_signal(bar, inc=1, device_id=(n, lax.rem(e + i, NE)), device_id_type=MESH)
    for i in range(1, NN):
        pl.semaphore_signal(bar, inc=1, device_id=(lax.rem(n + i, NN), e), device_id_type=MESH)
    for tn in (up, down):
        for te in (left, right):
            pl.semaphore_signal(bar, inc=1, device_id=(tn, te), device_id_type=MESH)
    load_g.wait()
    sent = exchange(pick, gates, s0, s1, m0, m1, rows, asem, arem, bar,
                    lambda: tables(win_v, feed_v, proj, taps, hot2, t1, t2, projq, wall))

    def put(i, v):
        ext[0, i + HALO] = v
        fbuf[i * CHANNELS:(i + 1) * CHANNELS, :] = v.astype(F32)

    blend(feed_s, rows, wbuf, share, grid, hot2, t1, t2, projq, load_w.wait, put)
    conv(rates, wall, out, ext, edges, halo, ybuf, fbuf, ssem, rsem)
    sent()


def per_device(gates, mixing_weight_blocks, send_pick, feed, window, proj_weight, conv_weight, rates):
    vm, sm = pl.BlockSpec(memory_space=pltpu.VMEM), pl.BlockSpec(memory_space=pltpu.SMEM)
    hbm = pl.BlockSpec(memory_space=pl.ANY)
    blk = (FEATS, GATES)
    return pl.pallas_call(
        kernel,
        out_shape=jax.ShapeDtypeStruct((CHANNELS, HR, HC), BF),
        in_specs=[sm, sm, sm, vm, vm, hbm, hbm, vm, vm],
        out_specs=vm,
        scratch_shapes=[
            pltpu.VMEM((NE, NN) + blk, BF), pltpu.VMEM((NN, NE) + blk, BF),
            pltpu.VMEM((NE, NN) + blk, BF), pltpu.VMEM((NN, NE) + blk, BF),
            pltpu.VMEM((2, ND) + blk, BF), pltpu.VMEM((PMAX,) + blk, BF),
            pltpu.VMEM((PMAX, GATES, 128), BF),
            pltpu.VMEM((PMAX * FEATS, 128), F32),
            pltpu.VMEM((128 * FEATS, 128), F32),
            pltpu.VMEM((128, 512), BF), pltpu.VMEM((512, 512), BF), pltpu.VMEM((512, 512), BF),
            pltpu.VMEM((CHANNELS, 64), BF), pltpu.VMEM((LAYERS, 3 * CHANNELS, 3 * CHANNELS), BF),
            pltpu.VMEM((LAYERS, ER, CHANNELS, HC), BF),
            pltpu.VMEM((LAYERS, 2, CHANNELS, HC), BF),
            pltpu.VMEM((LAYERS, 6, CHANNELS, HC), BF),
            pltpu.VMEM((ER, 3 * CHANNELS, HC), F32),
            pltpu.VMEM((HR * CHANNELS, HC), F32),
            pltpu.SemaphoreType.DMA((4,)), pltpu.SemaphoreType.DMA((4,)),
            pltpu.SemaphoreType.DMA((LAYERS,)), pltpu.SemaphoreType.DMA((LAYERS,)),
            pltpu.SemaphoreType.DMA((2,)),
        ],
        compiler_params=pltpu.CompilerParams(
            collective_id=0, has_side_effects=True, vmem_limit_bytes=58 << 20),
        name="radar",
    )(send_pick.transpose(0, 2, 1), feed, rates, feed, window, gates, mixing_weight_blocks, proj_weight, conv_weight)


def solution(mesh):
    in_specs = (
        P(("north", "east"), None, None),
        P(("north", "east"), None, None),
        P(("north", "east"), None, None),
        P(("north", "east"), None),
        P(("north", "east"), None),
        P(),
        P(),
        P(),
    )
    return jax.shard_map(
        per_device, mesh=mesh, in_specs=in_specs, out_specs=P(None, "north", "east"), check_vma=False
    )
```

time: 72.3 us -> 62.4 us (0.86)
  local copies, waits for them, and re-layouts: 9.34 us -> 1.87 us
  Pallas kernels: 62.4 us -> 60.3 us
    unnamed x15 -> x1, local copies, waits for them, and re-layouts: 8.37 us -> 1.87 us
    pallas_call x3 -> x1, Pallas kernels: 62.4 us -> 60.3 us  [per_device(): pl.pallas_call(kernel, out_shape=jax.ShapeDtypeStruct((CHANNELS, HR, HC),...]
    reshape x4 -> x0, local copies, waits for them, and re-layouts: 0.96 us -> none  [the longest x1 0.38 us: per_device(): conv_weight.reshape(LAYERS, 3, 3, CHANNELS, CHANNELS)]
where the time goes in v1:
time: 62.4 us; the launch traced here: 62.2 us
  Pallas kernels  60.3 us (97%)
  local copies, waits for them, and re-layouts  1.87 us (3%)
    pallas_call x1, Pallas kernels, per_device(): pl.pallas_call(kernel, out_shape=jax.ShapeDtypeStruct((CHANNELS, HR, HC),...  60.3 us
    unnamed x1, local copies, waits for them, and re-layouts  1.87 us

profile of v1, /device:TPU:1, one launch (start us, length us, event | category | flops | bytes accessed | tf_op | source)
XLA Modules:
  0.0 62.2 jit_solution(1326832900683234132)
XLA Ops:
  0.0 60.3 %radar.1 = bf16[64,32,128]{2,1,0:T(8,128)(2,1)} custom-call(s32[1,2,128]{2,1,0:T(2,128)} %bitcast.1, s32[1,256]{1,0:T(1,128)} %feed_v.1, s32[3]{0:T(128)} %rates.1, s32[1,256]{1,0:T(1,128)} %feed_v.1, s32[1,256]{1,0:T(1,128)} %win_v.1, bf16[256,16,128]{2,1,0:T(8,128)(2,1)} %gates_hbm.1, bf16[256,128,128]{2,1,0:T(8,128)(2,1)} %w_hbm.1, bf16[64,64]{1,0:T(8,128)(2,1)} %proj.1, ...), custom_call_target="tpu_custom_call" | custom-call | tf_op jit(solution)/shard_map/radar/pallas_call | solution.py:284
  60.3 1.9 %copy.10 = bf16[64,32,128]{2,1,0:T(8,128)(2,1)} copy(bf16[64,32,128]{2,1,0:T(8,128)(2,1)} %radar.1) | data formatting | bytes 1048576

commit v2 on v1

--- a/solution.py
+++ b/solution.py
@@ -22,7 +22,9 @@
 
 NCH = 8
 CH = PMAX // NCH
-ER = HR + 2 * HALO
+REACH = LAYERS * HALO
+ROWS = HR + 2 * REACH
+TILES, OFF, SPLIT = 36, 20, 28
 
 
 def iota(shape, dim):
@@ -125,7 +127,7 @@
         return carry
 
     wait_w()
-    lax.fori_loop(0, PMAX, product, 0, unroll=16)
+    lax.fori_loop(0, PMAX, product, 0, unroll=64)
     for f in range(0, FEATS, 2):
         parts = []
         for g in (f, f + 1):
@@ -163,94 +165,142 @@
             put(wr * 4 + i, o[:, i * 128:(i + 1) * 128])
 
 
-def conv(rates, wall, out, ext, edges, halo, ybuf, fbuf, ssem, rsem):
+def conv(rates, wall, out, xs, es, strips, halo, ybuf, ye, fbuf, ssem, rsem):
     n, e, up, down, left, right = places()
     lane = iota((CHANNELS, HC), 1)
-    row_ok = [(n > 0), None, (n < NN - 1)]
-    col_ok = [(e > 0), (e < NE - 1)]
-
-    def pack(layer, get):
-        el = jnp.zeros((CHANNELS, HC), F32)
-        er = jnp.zeros((CHANNELS, HC), F32)
-        for r in range(HR):
-            v = get(r)
-            here = (lane // HALO) == r
-            el = jnp.where(here, pltpu.roll(v, 4 * r, 1) if r else v, el)
-            er = jnp.where(here, pltpu.roll(v, (4 * r + 4) % 128, 1) if r < HR - 1 else v, er)
-        edges[layer, 0] = el.astype(BF)
-        edges[layer, 1] = er.astype(BF)
+    row_lane = iota((1, HC), 1)
+    zero = jnp.zeros((CHANNELS, HC), BF)
+
+    def remote(src, dst, dev):
+        pltpu.make_async_remote_copy(
+            src_ref=src, dst_ref=dst, send_sem=ssem.at[0], recv_sem=rsem.at[0],
+            device_id=dev, device_id_type=MESH).start()
+
+    for g in range(HR // 8):
+        sl, sr = zero, zero
+        for k in range(8):
+            v = xs[0, REACH + 8 * g + k]
+            here = lane // 16 == k
+            sl = jnp.where(here, pltpu.roll(v, 16 * k, 1) if k else v, sl)
+            sr = jnp.where(here, pltpu.roll(v, (16 * k + 16) % HC, 1) if k < 7 else v, sr)
+        strips[0, g] = sl
+        strips[1, g] = sr
+    for side, te in ((0, right), (1, left)):
+        own = strips.at[1 - side]
+        remote(own, halo.at[side, pl.ds(2, 4)], (n, te))
+        remote(own.at[pl.ds(2, 2)], halo.at[side, pl.ds(0, 2)], (down, te))
+        remote(own.at[pl.ds(0, 2)], halo.at[side, pl.ds(6, 2)], (up, te))
+    remote(xs.at[0, pl.ds(REACH, REACH)], xs.at[0, pl.ds(REACH + HR, REACH)], (up, e))
+    remote(xs.at[0, pl.ds(HR, REACH)], xs.at[0, pl.ds(0, REACH)], (down, e))
+    arrived = xs.at[0, pl.ds(0, 2 * REACH + 16)]
+    pltpu.make_async_copy(arrived, arrived, rsem.at[0]).wait()
+
+    @pl.when(n == 0)
+    def _():
+        xs[0, pl.ds(0, REACH)] = jnp.zeros((REACH, CHANNELS, HC), BF)
+
+    @pl.when(n == NN - 1)
+    def _():
+        xs[0, pl.ds(REACH + HR, REACH)] = jnp.zeros((REACH, CHANNELS, HC), BF)
+
+    up_ok, down_ok = jnp.where(n > 0, 1.0, 0.0), jnp.where(n < NN - 1, 1.0, 0.0)
+    left_ok, right_ok = jnp.where(e > 0, 1.0, 0.0), jnp.where(e < NE - 1, 1.0, 0.0)
+    part = row_lane % 64
+    cols = jnp.where(part < 16, left_ok, jnp.where(part >= 48, right_ok, 1.0))
+
+    def edge_mask(t):
+        first = jnp.where(t < REACH, up_ok, 1.0)
+        second = jnp.where(t + OFF >= REACH + HR, down_ok, 1.0)
+        return cols * jnp.where(row_lane < 64, first, second)
+
+    def assemble(t, carry):
+        h0, o0 = (t + 4) // 8, lax.rem(t + 4, 8)
+        h1, o1 = (t + OFF + 4) // 8, lax.rem(t + OFF + 4, 8)
+        a, b = xs[0, t], xs[0, t + OFF]
+        pieces = [
+            pltpu.roll(halo[0, h0], lax.rem(HC - 16 * o0, HC), 1), pltpu.roll(a, 16, 1),
+            pltpu.roll(a, 48, 1), pltpu.roll(halo[1, h0], lax.rem(HC + 48 - 16 * o0, HC), 1),
+            pltpu.roll(halo[0, h1], lax.rem(HC + 64 - 16 * o1, HC), 1), pltpu.roll(b, 80, 1),
+            pltpu.roll(b, 112, 1), pltpu.roll(halo[1, h1], lax.rem(HC + 112 - 16 * o1, HC), 1),
+        ]
+        v = pieces[0]
+        for k in range(1, 8):
+            v = jnp.where(lane // 16 == k, pieces[k], v)
+        es[0, t] = (v.astype(F32) * edge_mask(t)).astype(BF)
+        return carry
+
+    lax.fori_loop(0, TILES, assemble, 0, unroll=12)
 
     for layer in range(LAYERS):
-        pack(layer, lambda r: fbuf[r * CHANNELS:(r + 1) * CHANNELS, :])
-
-        def remote(src, dst, dev):
-            cp = pltpu.make_async_remote_copy(
-                src_ref=src, dst_ref=dst, send_sem=ssem.at[layer], recv_sem=rsem.at[layer],
-                device_id=dev, device_id_type=MESH)
-            cp.start()
-
-        remote(ext.at[layer, pl.ds(HALO, HALO)], ext.at[layer, pl.ds(HALO + HR, HALO)], (up, e))
-        remote(ext.at[layer, pl.ds(HR, HALO)], ext.at[layer, pl.ds(0, HALO)], (down, e))
-        for k, tn in ((2, up), (1, n), (0, down)):
-            remote(edges.at[layer, 1], halo.at[layer, k], (tn, right))
-            remote(edges.at[layer, 0], halo.at[layer, 3 + k], (tn, left))
-        everything = ext.at[layer, pl.ds(0, 14)]
-        pltpu.make_async_copy(everything, everything, rsem.at[layer]).wait()
-
         d = rates[layer]
         w = wall[layer]
-
-        def one_row(m, k, rr):
-            x = ext[layer, m].astype(F32)
-            lt = halo[layer, k].astype(F32)
-            rt = halo[layer, 3 + k].astype(F32)
-            ok = row_ok[k]
-            if ok is not None:
-                x = jnp.where(ok, x, 0.0)
-            okl = col_ok[0] if ok is None else jnp.logical_and(ok, col_ok[0])
-            okr = col_ok[1] if ok is None else jnp.logical_and(ok, col_ok[1])
-            lt = jnp.where(okl, lt, 0.0)
-            rt = jnp.where(okr, rt, 0.0)
-            lt = pltpu.roll(lt, lax.rem(d + 124 - 4 * rr + 128, 128), 1)
+        lo = HALO * layer
+
+        def one_row(m, second):
+            x = xs[layer, m]
+            edge = es[layer, m - OFF if second else m]
+            lt = pltpu.roll(edge, d + (48 if second else 112), 1)
+            rt = pltpu.roll(edge, (16 if second else 80) - d, 1)
             xl = jnp.where(lane >= d, pltpu.roll(x, d, 1), lt)
-            rt = pltpu.roll(rt, lax.rem(256 - d - 4 * rr, 128), 1)
             xr = jnp.where(lane < HC - d, pltpu.roll(x, HC - d, 1), rt)
-            return jnp.concatenate([xl.astype(BF), x.astype(BF), xr.astype(BF)], axis=0)
-
-        def two_rows(m, k, rr):
-            b = jnp.concatenate([one_row(m, k, rr), one_row(m + 1, k, rr + 1)], axis=1)
+            return jnp.concatenate([xl, x, xr], axis=0)
+
+        def two_rows(first, second, i, carry):
+            m = first + 2 * i
+            b = jnp.concatenate([one_row(m, second), one_row(m + 1, second)], axis=1)
             y = jnp.dot(w, b, preferred_element_type=F32)
             ybuf[m] = y[:, :HC]
             ybuf[m + 1] = y[:, HC:]
-
-        for m in (0, 2):
-            two_rows(m, 0, HR - HALO + m)
-        lax.fori_loop(0, HR // 2, lambda i, c: (two_rows(HALO + 2 * i, 1, 2 * i), c)[1], 0, unroll=4)
-        for m in (0, 2):
-            two_rows(HALO + HR + m, 2, m)
-
-        def finish(i, carry):
-            h = (ybuf[i + HALO - d, 0:64, :] + ybuf[i + HALO, 64:128, :]
-                 + ybuf[i + HALO + d, 128:192, :])
-            at = pl.ds(pl.multiple_of(i * CHANNELS, CHANNELS), CHANNELS)
-            v = (fbuf[at, :] + jax.nn.gelu(h)).astype(BF)
-            fbuf[at, :] = v.astype(F32)
+            return carry
+
+        def one_edge(t):
+            x = es[layer, t]
+            return jnp.concatenate([pltpu.roll(x, d, 1), x, pltpu.roll(x, HC - d, 1)], axis=0)
+
+        def two_edges(i, carry):
+            t = lo + 2 * i
+            b = jnp.concatenate([one_edge(t), one_edge(t + 1)], axis=1)
+            y = jnp.dot(w, b, preferred_element_type=F32)
+            ye[t] = y[:, :HC]
+            ye[t + 1] = y[:, HC:]
+            return carry
+
+        count = (SPLIT - lo) // 2
+        lax.fori_loop(0, count, functools.partial(two_rows, lo, False), 0, unroll=count)
+        lax.fori_loop(0, count, functools.partial(two_rows, SPLIT, True), 0, unroll=count)
+        if layer < LAYERS - 1:
+            lax.fori_loop(0, (TILES - 2 * lo) // 2, two_edges, 0, unroll=(TILES - 2 * lo) // 2)
+        new = lo + HALO
+
+        def total(buf, m):
+            return buf[m - d, 0:64, :] + buf[m, 64:128, :] + buf[m + d, 128:192, :]
+
+        def finish(m, carry):
+            v = xs[layer, m].astype(F32) + jax.nn.gelu(total(ybuf, m))
             if layer < LAYERS - 1:
-                ext[layer + 1, i + HALO] = v
+                v = v * jnp.where(m < REACH, up_ok, jnp.where(m >= REACH + HR, down_ok, 1.0))
+                xs[layer + 1, m] = v.astype(BF)
+            else:
+                fbuf[pl.ds(pl.multiple_of((m - REACH) * CHANNELS, CHANNELS), CHANNELS), :] = v
             return carry
 
-        lax.fori_loop(0, HR, finish, 0, unroll=4)
+        def finish_edge(t, carry):
+            v = (es[layer, t].astype(F32) + jax.nn.gelu(total(ye, t))) * edge_mask(t)
+            es[layer + 1, t] = v.astype(BF)
+            return carry
+
+        lax.fori_loop(new, ROWS - new, finish, 0, unroll=8)
+        if layer < LAYERS - 1:
+            lax.fori_loop(new, TILES - new, finish_edge, 0, unroll=4)
 
     for c in range(CHANNELS):
         out[c] = fbuf[pl.ds(c, HR, stride=CHANNELS), :].astype(BF)
-    for layer in range(LAYERS):
-        everything = ext.at[layer, pl.ds(0, 14)]
-        pltpu.make_async_copy(everything, everything, ssem.at[layer]).wait()
+    pltpu.make_async_copy(arrived, arrived, ssem.at[0]).wait()
 
 
 def kernel(pick, feed_s, rates, feed_v, win_v, gates_hbm, w_hbm, proj, taps, out,
            s0, s1, m0, m1, rows, gates, wbuf, share, grid, hot2, t1, t2, projq, wall,
-           ext, edges, halo, ybuf, fbuf, asem, arem, ssem, rsem, lsem):
+           xs, es, strips, halo, ybuf, ye, fbuf, asem, arem, ssem, rsem, lsem):
     n, e, up, down, left, right = places()
     load_g = pltpu.make_async_copy(gates_hbm, gates, lsem.at[0])
     load_g.start()
@@ -269,11 +319,10 @@
                     lambda: tables(win_v, feed_v, proj, taps, hot2, t1, t2, projq, wall))
 
     def put(i, v):
-        ext[0, i + HALO] = v
-        fbuf[i * CHANNELS:(i + 1) * CHANNELS, :] = v.astype(F32)
+        xs[0, i + REACH] = v
 
     blend(feed_s, rows, wbuf, share, grid, hot2, t1, t2, projq, load_w.wait, put)
-    conv(rates, wall, out, ext, edges, halo, ybuf, fbuf, ssem, rsem)
+    conv(rates, wall, out, xs, es, strips, halo, ybuf, ye, fbuf, ssem, rsem)
     sent()
 
 
@@ -295,13 +344,15 @@
             pltpu.VMEM((128 * FEATS, 128), F32),
             pltpu.VMEM((128, 512), BF), pltpu.VMEM((512, 512), BF), pltpu.VMEM((512, 512), BF),
             pltpu.VMEM((CHANNELS, 64), BF), pltpu.VMEM((LAYERS, 3 * CHANNELS, 3 * CHANNELS), BF),
-            pltpu.VMEM((LAYERS, ER, CHANNELS, HC), BF),
-            pltpu.VMEM((LAYERS, 2, CHANNELS, HC), BF),
-            pltpu.VMEM((LAYERS, 6, CHANNELS, HC), BF),
-            pltpu.VMEM((ER, 3 * CHANNELS, HC), F32),
+            pltpu.VMEM((LAYERS, ROWS, CHANNELS, HC), BF),
+            pltpu.VMEM((LAYERS, TILES, CHANNELS, HC), BF),
+            pltpu.VMEM((2, HR // 8, CHANNELS, HC), BF),
+            pltpu.VMEM((2, 8, CHANNELS, HC), BF),
+            pltpu.VMEM((ROWS, 3 * CHANNELS, HC), F32),
+            pltpu.VMEM((TILES, 3 * CHANNELS, HC), F32),
             pltpu.VMEM((HR * CHANNELS, HC), F32),
             pltpu.SemaphoreType.DMA((4,)), pltpu.SemaphoreType.DMA((4,)),
-            pltpu.SemaphoreType.DMA((LAYERS,)), pltpu.SemaphoreType.DMA((LAYERS,)),
+            pltpu.SemaphoreType.DMA((1,)), pltpu.SemaphoreType.DMA((1,)),
             pltpu.SemaphoreType.DMA((2,)),
         ],
         compiler_params=pltpu.CompilerParams(

time: 62.4 us -> 51 us (0.82)
  Pallas kernels: 60.3 us -> 48.9 us
    pallas_call x1, Pallas kernels: 60.3 us -> 48.9 us  [per_device(): pl.pallas_call(kernel, out_shape=jax.ShapeDtypeStruct((CHANNELS, HR, HC),...]
where the time goes in v2:
time: 51 us; the launch traced here: 50.8 us
  Pallas kernels  48.9 us (96%)
  local copies, waits for them, and re-layouts  1.87 us (4%)
    pallas_call x1, Pallas kernels, per_device(): pl.pallas_call(kernel, out_shape=jax.ShapeDtypeStruct((CHANNELS, HR, HC),...  48.9 us
    unnamed x1, local copies, waits for them, and re-layouts  1.87 us

profile of v2, /device:TPU:1, one launch (start us, length us, event | category | flops | bytes accessed | tf_op | source)
XLA Modules:
  0.0 50.8 jit_solution(3741776138648687546)
XLA Ops:
  0.0 48.9 %radar.1 = bf16[64,32,128]{2,1,0:T(8,128)(2,1)} custom-call(s32[1,2,128]{2,1,0:T(2,128)} %bitcast.1, s32[1,256]{1,0:T(1,128)} %feed_v.1, s32[3]{0:T(128)} %rates.1, s32[1,256]{1,0:T(1,128)} %feed_v.1, s32[1,256]{1,0:T(1,128)} %win_v.1, bf16[256,16,128]{2,1,0:T(8,128)(2,1)} %gates_hbm.1, bf16[256,128,128]{2,1,0:T(8,128)(2,1)} %w_hbm.1, bf16[64,64]{1,0:T(8,128)(2,1)} %proj.1, ...), custom_call_target="tpu_custom_call" | custom-call | tf_op jit(solution)/shard_map/radar/pallas_call | solution.py:333
  48.9 1.9 %copy.10 = bf16[64,32,128]{2,1,0:T(8,128)(2,1)} copy(bf16[64,32,128]{2,1,0:T(8,128)(2,1)} %radar.1) | data formatting | bytes 1048576

commit v3 on v2

--- a/solution.py
+++ b/solution.py
@@ -38,68 +38,84 @@
     return n, e, up, down, left, right
 
 
-def exchange(pick, gates, s0, s1, m0, m1, rows, ssem, rsem, bar, meanwhile):
+def exchange(pick, gates, s0, s1, m0, m1, rows, ssem, rsem, bar, meanwhile, arrived):
     n, e, up, down, left, right = places()
-    peers_e = [lax.rem(e + i, NE) for i in range(1, NE)]
-    peers_n = [lax.rem(n + i, NN) for i in range(1, NN)]
+    f0, f1 = rows.at[0], rows.at[1]
 
     def gather(t, carry):
-        tn, te = t // NE, lax.rem(t, NE)
+        i, j = t // NE, lax.rem(t, NE)
+        at = lax.rem(n + i, NN) * NE + lax.rem(e + j, NE)
         for k in range(2):
-            p = pick[0, k, t]
+            p = pick[0, k, at]
             v = gates[jnp.maximum(p, 0)]
             v = jnp.where(p >= 0, v, jnp.zeros_like(v))
             if k == 0:
-                s0[te, tn] = v
+                s0[j, i] = v
             else:
-                s1[tn, te] = v
+                s1[i, j] = v
         return carry
 
-    lax.fori_loop(0, ND, gather, 0, unroll=8)
+    lax.fori_loop(0, ND, gather, 0, unroll=16)
     pl.semaphore_wait(bar, NE + NN - 2 + 4)
-    f0, f1 = rows.at[0], rows.at[1]
-
-    def remote(src, dst, k, dev):
-        return pltpu.make_async_remote_copy(
+
+    def remote(src, dst, k, i, j):
+        pltpu.make_async_remote_copy(
             src_ref=src, dst_ref=dst, send_sem=ssem.at[k], recv_sem=rsem.at[k],
-            device_id=dev, device_id_type=MESH,
-        )
-
-    for i in range(NE - 1):
-        remote(s0.at[peers_e[i]], m0.at[e], 0, (n, peers_e[i])).start()
-        if i < NN - 1:
-            remote(s1.at[peers_n[i]], m1.at[n], 1, (peers_n[i], e)).start()
-    m0[e] = s0[e]
-    m1[n] = s1[n]
+            device_id=(lax.rem(n + i, NN), lax.rem(e + j, NE)), device_id_type=MESH,
+        ).start()
+
+    for c in range(2):
+        for j in range(max(1, 8 * c), 8 * c + 8):
+            remote(s0.at[j], m0.at[j], c, 0, j)
+            i = j // 2
+            if j % 2 == 0 and i > 0:
+                remote(s1.at[i], m1.at[i], 2 + c, i, 0)
+    m0[0] = s0[0]
+    m1[0] = s1[0]
     meanwhile()
 
-    def wait(ref, count, sem):
-        r = ref.at[pl.ds(0, count)]
+    def wait(count, sem):
+        r = rows.at[0, pl.ds(0, count)]
         pltpu.make_async_copy(r, r, sem).wait()
 
-    wait(m1, NN - 1, rsem.at[1])
-    for te in peers_e:
-        remote(m1.at[:, te], f1.at[pl.ds(e * NN, NN)], 3, (n, te)).start()
-    f1[pl.ds(e * NN, NN)] = m1[:, e]
-    wait(m0, NE - 1, rsem.at[0])
-    for tn in peers_n:
-        remote(m0.at[:, tn], f0.at[pl.ds(n * NE, NE)], 2, (tn, e)).start()
-    f0[pl.ds(n * NE, NE)] = m0[:, n]
-    wait(f1, ND - NN, rsem.at[3])
-    wait(f0, ND - NE, rsem.at[2])
+    a_counts = (7 * NN, 8 * NN, 3 * NE, 4 * NE)
+    b_counts = (7 * 8, 7 * 8, 15 * 4, 15 * 4)
+    for c in range(2):
+        wait(a_counts[2 + c], rsem.at[2 + c])
+        for j in range(1, NE):
+            remote(m1.at[pl.ds(4 * c, 4), j], f1.at[pl.ds(j * NN + 4 * c, 4)], 6 + c, 0, j)
+        f1[pl.ds(4 * c, 4)] = m1[pl.ds(4 * c, 4), 0]
+        wait(a_counts[c], rsem.at[c])
+        for i in range(1, NN):
+            remote(m0.at[pl.ds(8 * c, 8), i], f0.at[pl.ds(i * NE + 8 * c, 8)], 4 + c, i, 0)
+        f0[pl.ds(8 * c, 8)] = m0[pl.ds(8 * c, 8), 0]
+    for c in range(2):
+        for k in (1, 0):
+            wait(b_counts[2 * k + c], rsem.at[4 + 2 * k + c])
+            arrived(k, c)
 
     def sent():
-        wait(m0, NE - 1, ssem.at[0])
-        wait(m1, NN - 1, ssem.at[1])
-        wait(f0, ND - NE, ssem.at[2])
-        wait(f1, ND - NN, ssem.at[3])
+        for k, count in enumerate(a_counts + b_counts):
+            wait(count, ssem.at[k])
 
     return sent
 
 
-def tables(win_v, feed_v, proj, taps, hot2, t1, t2, projq, wall):
-    hot = (win_v[...] == iota((GATES, PMAX), 0)) & (feed_v[...] >= 0)
-    hot = jnp.where(hot, 1.0, 0.0).astype(BF)
+def tables(win_v, feed_v, proj, taps, hot2, t1, t2, projq, wall, entry):
+    n, e, *_ = places()
+    feed = feed_v[...]
+    s, k = feed // 2, feed % 2
+    i, j = (n + NN - s // NE) % NN, (e + NE - s % NE) % NE
+    q = jnp.where(feed < 0, -1, jnp.where(k == 0, i * NE + j, ND + j * NN + i))
+    down_q = jnp.transpose(jnp.broadcast_to(q, (128, PMAX)))
+    number = iota((PMAX, 128), 0)
+    uses = []
+    for h in range(2):
+        same = down_q == iota((PMAX, 128), 1) + 128 * h
+        entry[:, h * 128:(h + 1) * 128] = jnp.max(jnp.where(same, number, 0), axis=0, keepdims=True)
+        uses.append(jnp.where(same, 1.0, 0.0).astype(BF))
+    hot = jnp.where(win_v[...] == iota((GATES, PMAX), 0), 1.0, 0.0).astype(BF)
+    hot = jnp.dot(hot, jnp.concatenate(uses, axis=1), preferred_element_type=F32).astype(BF)
     hot2[...] = jnp.concatenate([hot, hot], axis=1)
     col = iota((1, 512), 1)
     i1, w1, a1, b1, j1 = col // 128, col // 32 % 4, col // 16 % 2, col // 8 % 2, col % 8
@@ -117,17 +133,18 @@
             wall[layer, a * CHANNELS:(a + 1) * CHANNELS, :] = jnp.concatenate(line, axis=1).astype(BF)
 
 
-def blend(feed_s, rows, wbuf, share, grid, hot2, t1, t2, projq, wait_w, put):
-    def product(p, carry):
-        j = jnp.maximum(feed_s[0, p], 0)
-        s, k = j // 2, lax.rem(j, 2)
-        q = jnp.where(k == 0, s, lax.rem(s, NE) * NN + s // NE)
-        share[pl.ds(pl.multiple_of(p * FEATS, FEATS), FEATS), :] = jnp.dot(
-            rows[k, q], wbuf[p], preferred_element_type=F32)
+def products(k, c, entry, rows, wbuf, share):
+    def product(t, carry):
+        q = t // 8 * NE + 8 * c + lax.rem(t, 8) if k == 0 else t // 4 * NN + 4 * c + lax.rem(t, 4)
+        at = pl.multiple_of((k * ND + q) * FEATS, FEATS)
+        share[pl.ds(at, FEATS), :] = jnp.dot(
+            rows[k, q], wbuf[entry[0, k * ND + q]], preferred_element_type=F32)
         return carry
 
-    wait_w()
-    lax.fori_loop(0, PMAX, product, 0, unroll=64)
+    lax.fori_loop(0, 64, product, 0, unroll=64)
+
+
+def blend(share, grid, hot2, t1, t2, projq, put):
     for f in range(0, FEATS, 2):
         parts = []
         for g in (f, f + 1):
@@ -298,14 +315,15 @@
     pltpu.make_async_copy(arrived, arrived, ssem.at[0]).wait()
 
 
-def kernel(pick, feed_s, rates, feed_v, win_v, gates_hbm, w_hbm, proj, taps, out,
+def kernel(pick_h, feed_h, rates_h, win_h, gates_h, w_h, proj_h, taps_h, out,
            s0, s1, m0, m1, rows, gates, wbuf, share, grid, hot2, t1, t2, projq, wall,
-           xs, es, strips, halo, ybuf, ye, fbuf, asem, arem, ssem, rsem, lsem):
+           xs, es, strips, halo, ybuf, ye, fbuf, pick, entry, entry_v, rates, feed_v, win_v, proj, taps,
+           asem, arem, ssem, rsem, lsem):
     n, e, up, down, left, right = places()
-    load_g = pltpu.make_async_copy(gates_hbm, gates, lsem.at[0])
-    load_g.start()
-    load_w = pltpu.make_async_copy(w_hbm, wbuf, lsem.at[1])
-    load_w.start()
+    pairs = [(pick_h, pick), (gates_h, gates), (rates_h, rates), (feed_h, feed_v), (win_h, win_v), (proj_h, proj), (taps_h, taps), (w_h, wbuf)]
+    loads = [pltpu.make_async_copy(src, dst, lsem.at[k]) for k, (src, dst) in enumerate(pairs)]
+    for load in loads:
+        load.start()
     bar = pltpu.get_barrier_semaphore()
     for i in range(1, NE):
         pl.semaphore_signal(bar, inc=1, device_id=(n, lax.rem(e + i, NE)), device_id_type=MESH)
@@ -314,27 +332,37 @@
     for tn in (up, down):
         for te in (left, right):
             pl.semaphore_signal(bar, inc=1, device_id=(tn, te), device_id_type=MESH)
-    load_g.wait()
-    sent = exchange(pick, gates, s0, s1, m0, m1, rows, asem, arem, bar,
-                    lambda: tables(win_v, feed_v, proj, taps, hot2, t1, t2, projq, wall))
+    loads[0].wait()
+    loads[1].wait()
+
+    def meanwhile():
+        for load in loads[2:7]:
+            load.wait()
+        tables(win_v, feed_v, proj, taps, hot2, t1, t2, projq, wall, entry_v)
+        to_scalar = pltpu.make_async_copy(entry_v, entry, lsem.at[8])
+        to_scalar.start()
+        to_scalar.wait()
+        loads[7].wait()
+
+    sent = exchange(pick, gates, s0, s1, m0, m1, rows, asem, arem, bar, meanwhile,
+                    lambda k, c: products(k, c, entry, rows, wbuf, share))
 
     def put(i, v):
         xs[0, i + REACH] = v
 
-    blend(feed_s, rows, wbuf, share, grid, hot2, t1, t2, projq, load_w.wait, put)
+    blend(share, grid, hot2, t1, t2, projq, put)
     conv(rates, wall, out, xs, es, strips, halo, ybuf, ye, fbuf, ssem, rsem)
     sent()
 
 
 def per_device(gates, mixing_weight_blocks, send_pick, feed, window, proj_weight, conv_weight, rates):
-    vm, sm = pl.BlockSpec(memory_space=pltpu.VMEM), pl.BlockSpec(memory_space=pltpu.SMEM)
-    hbm = pl.BlockSpec(memory_space=pl.ANY)
+    hbm = pl.BlockSpec(memory_space=pltpu.HBM)
     blk = (FEATS, GATES)
     return pl.pallas_call(
         kernel,
         out_shape=jax.ShapeDtypeStruct((CHANNELS, HR, HC), BF),
-        in_specs=[sm, sm, sm, vm, vm, hbm, hbm, vm, vm],
-        out_specs=vm,
+        in_specs=[hbm] * 8,
+        out_specs=pl.BlockSpec(memory_space=pltpu.VMEM),
         scratch_shapes=[
             pltpu.VMEM((NE, NN) + blk, BF), pltpu.VMEM((NN, NE) + blk, BF),
             pltpu.VMEM((NE, NN) + blk, BF), pltpu.VMEM((NN, NE) + blk, BF),
@@ -351,14 +379,17 @@
             pltpu.VMEM((ROWS, 3 * CHANNELS, HC), F32),
             pltpu.VMEM((TILES, 3 * CHANNELS, HC), F32),
             pltpu.VMEM((HR * CHANNELS, HC), F32),
-            pltpu.SemaphoreType.DMA((4,)), pltpu.SemaphoreType.DMA((4,)),
+            pltpu.SMEM((1, 2, ND), jnp.int32), pltpu.SMEM((1, PMAX), jnp.int32), pltpu.VMEM((1, PMAX), jnp.int32),
+            pltpu.SMEM((LAYERS,), jnp.int32), pltpu.VMEM((1, PMAX), jnp.int32), pltpu.VMEM((1, PMAX), jnp.int32),
+            pltpu.VMEM((CHANNELS, 64), BF), pltpu.VMEM((LAYERS, 9, CHANNELS, CHANNELS), BF),
+            pltpu.SemaphoreType.DMA((8,)), pltpu.SemaphoreType.DMA((8,)),
             pltpu.SemaphoreType.DMA((1,)), pltpu.SemaphoreType.DMA((1,)),
-            pltpu.SemaphoreType.DMA((2,)),
+            pltpu.SemaphoreType.DMA((9,)),
         ],
         compiler_params=pltpu.CompilerParams(
             collective_id=0, has_side_effects=True, vmem_limit_bytes=58 << 20),
         name="radar",
-    )(send_pick.transpose(0, 2, 1), feed, rates, feed, window, gates, mixing_weight_blocks, proj_weight, conv_weight)
+    )(send_pick.transpose(0, 2, 1), feed, rates, window, gates, mixing_weight_blocks, proj_weight, conv_weight)
 
 
 def solution(mesh):

time: 51 us -> 45.8 us (0.90)
  Pallas kernels: 48.9 us -> 43.8 us
    pallas_call x1, Pallas kernels: 48.9 us -> 43.8 us  [per_device(): pl.pallas_call(kernel, out_shape=jax.ShapeDtypeStruct((CHANNELS, HR, HC),...]
where the time goes in v3:
time: 45.8 us; the launch traced here: 45.6 us
  Pallas kernels  43.8 us (96%)
  local copies, waits for them, and re-layouts  1.87 us (4%)
    pallas_call x1, Pallas kernels, per_device(): pl.pallas_call(kernel, out_shape=jax.ShapeDtypeStruct((CHANNELS, HR, HC),...  43.8 us
    unnamed x1, local copies, waits for them, and re-layouts  1.87 us

profile of v3, /device:TPU:1, one launch (start us, length us, event | category | flops | bytes accessed | tf_op | source)
XLA Modules:
  0.0 45.6 jit_solution(12258663727217441973)
XLA Ops:
  0.0 43.8 %radar.1 = bf16[64,32,128]{2,1,0:T(8,128)(2,1)} custom-call(s32[1,2,128]{2,1,0:T(2,128)} %bitcast.1, s32[1,256]{1,0:T(1,128)} %feed_h.1, s32[3]{0:T(128)} %rates_h.1, s32[1,256]{1,0:T(1,128)} %win_h.1, bf16[256,16,128]{2,1,0:T(8,128)(2,1)} %gates_h.1, bf16[256,128,128]{2,1,0:T(8,128)(2,1)} %w_h.1, bf16[64,64]{1,0:T(8,128)(2,1)} %proj_h.1, ...), custom_call_target="tpu_custom_call" | custom-call | tf_op jit(solution)/shard_map/radar/pallas_call | solution.py:361
  43.8 1.9 %copy.10 = bf16[64,32,128]{2,1,0:T(8,128)(2,1)} copy(bf16[64,32,128]{2,1,0:T(8,128)(2,1)} %radar.1) | data formatting | bytes 1048576

commit v4 on v3

--- a/solution.py
+++ b/solution.py
@@ -144,7 +144,7 @@
     lax.fori_loop(0, 64, product, 0, unroll=64)
 
 
-def blend(share, grid, hot2, t1, t2, projq, put):
+def blend(share, grid, hot2, t1, t2, projq, put, send):
     for f in range(0, FEATS, 2):
         parts = []
         for g in (f, f + 1):
@@ -180,45 +180,44 @@
         o = jax.nn.gelu(o).astype(BF)
         for i in range(4):
             put(wr * 4 + i, o[:, i * 128:(i + 1) * 128])
-
-
-def conv(rates, wall, out, xs, es, strips, halo, ybuf, ye, fbuf, ssem, rsem):
+        if wr % 2:
+            send(wr // 2)
+
+
+def send_halo(g, xs, strips, halo, ssem, rsem):
+    n, e, up, down, left, right = places()
+    lane = iota((CHANNELS, HC), 1)
+
+    def remote(src, dst, dev, k=0):
+        pltpu.make_async_remote_copy(
+            src_ref=src, dst_ref=dst, send_sem=ssem.at[k], recv_sem=rsem.at[k],
+            device_id=dev, device_id_type=MESH).start()
+
+    sl = sr = jnp.zeros((CHANNELS, HC), BF)
+    for k in range(8):
+        v = xs[0, REACH + 8 * g + k]
+        here = lane // 16 == k
+        sl = jnp.where(here, pltpu.roll(v, 16 * k, 1) if k else v, sl)
+        sr = jnp.where(here, pltpu.roll(v, (16 * k + 16) % HC, 1) if k < 7 else v, sr)
+    strips[0, g] = sl
+    strips[1, g] = sr
+    for side, te in ((0, right), (1, left)):
+        own = strips.at[1 - side, g]
+        remote(own, halo.at[side, g + 2], (n, te))
+        if g >= 2:
+            remote(own, halo.at[side, g - 2], (down, te))
+        else:
+            remote(own, halo.at[side, g + 6], (up, te))
+    if g == 1:
+        remote(xs.at[0, pl.ds(REACH, REACH)], xs.at[0, pl.ds(REACH + HR, REACH)], (up, e), 1)
+    if g == 3:
+        remote(xs.at[0, pl.ds(HR, REACH)], xs.at[0, pl.ds(0, REACH)], (down, e), 1)
+
+
+def conv(rates, wall, out, xs, es, halo, ybuf, ye, fbuf, ssem, rsem):
     n, e, up, down, left, right = places()
     lane = iota((CHANNELS, HC), 1)
     row_lane = iota((1, HC), 1)
-    zero = jnp.zeros((CHANNELS, HC), BF)
-
-    def remote(src, dst, dev):
-        pltpu.make_async_remote_copy(
-            src_ref=src, dst_ref=dst, send_sem=ssem.at[0], recv_sem=rsem.at[0],
-            device_id=dev, device_id_type=MESH).start()
-
-    for g in range(HR // 8):
-        sl, sr = zero, zero
-        for k in range(8):
-            v = xs[0, REACH + 8 * g + k]
-            here = lane // 16 == k
-            sl = jnp.where(here, pltpu.roll(v, 16 * k, 1) if k else v, sl)
-            sr = jnp.where(here, pltpu.roll(v, (16 * k + 16) % HC, 1) if k < 7 else v, sr)
-        strips[0, g] = sl
-        strips[1, g] = sr
-    for side, te in ((0, right), (1, left)):
-        own = strips.at[1 - side]
-        remote(own, halo.at[side, pl.ds(2, 4)], (n, te))
-        remote(own.at[pl.ds(2, 2)], halo.at[side, pl.ds(0, 2)], (down, te))
-        remote(own.at[pl.ds(0, 2)], halo.at[side, pl.ds(6, 2)], (up, te))
-    remote(xs.at[0, pl.ds(REACH, REACH)], xs.at[0, pl.ds(REACH + HR, REACH)], (up, e))
-    remote(xs.at[0, pl.ds(HR, REACH)], xs.at[0, pl.ds(0, REACH)], (down, e))
-    arrived = xs.at[0, pl.ds(0, 2 * REACH + 16)]
-    pltpu.make_async_copy(arrived, arrived, rsem.at[0]).wait()
-
-    @pl.when(n == 0)
-    def _():
-        xs[0, pl.ds(0, REACH)] = jnp.zeros((REACH, CHANNELS, HC), BF)
-
-    @pl.when(n == NN - 1)
-    def _():
-        xs[0, pl.ds(REACH + HR, REACH)] = jnp.zeros((REACH, CHANNELS, HC), BF)
 
     up_ok, down_ok = jnp.where(n > 0, 1.0, 0.0), jnp.where(n < NN - 1, 1.0, 0.0)
     left_ok, right_ok = jnp.where(e > 0, 1.0, 0.0), jnp.where(e < NE - 1, 1.0, 0.0)
@@ -230,7 +229,7 @@
         second = jnp.where(t + OFF >= REACH + HR, down_ok, 1.0)
         return cols * jnp.where(row_lane < 64, first, second)
 
-    def assemble(t, carry):
+    def assemble(t):
         h0, o0 = (t + 4) // 8, lax.rem(t + 4, 8)
         h1, o1 = (t + OFF + 4) // 8, lax.rem(t + OFF + 4, 8)
         a, b = xs[0, t], xs[0, t + OFF]
@@ -244,75 +243,113 @@
         for k in range(1, 8):
             v = jnp.where(lane // 16 == k, pieces[k], v)
         es[0, t] = (v.astype(F32) * edge_mask(t)).astype(BF)
-        return carry
-
-    lax.fori_loop(0, TILES, assemble, 0, unroll=12)
-
-    for layer in range(LAYERS):
+
+    def loop(lo, hi, body, unroll):
+        lax.fori_loop(lo, hi, lambda m, carry: (body(m), carry)[1], 0, unroll=unroll)
+
+    def total(buf, m, d):
+        return buf[m - d, 0:64, :] + buf[m, 64:128, :] + buf[m + d, 128:192, :]
+
+    def layer_ops(layer):
         d = rates[layer]
         w = wall[layer]
-        lo = HALO * layer
+        y_of = ybuf.at[layer % 2]
 
         def one_row(m, second):
             x = xs[layer, m]
-            edge = es[layer, m - OFF if second else m]
-            lt = pltpu.roll(edge, d + (48 if second else 112), 1)
-            rt = pltpu.roll(edge, (16 if second else 80) - d, 1)
+            if second is None:
+                lt = rt = jnp.zeros((CHANNELS, HC), BF)
+            else:
+                edge = es[layer, m - OFF if second else m]
+                lt = pltpu.roll(edge, d + (48 if second else 112), 1)
+                rt = pltpu.roll(edge, (16 if second else 80) - d, 1)
             xl = jnp.where(lane >= d, pltpu.roll(x, d, 1), lt)
             xr = jnp.where(lane < HC - d, pltpu.roll(x, HC - d, 1), rt)
             return jnp.concatenate([xl, x, xr], axis=0)
 
-        def two_rows(first, second, i, carry):
-            m = first + 2 * i
-            b = jnp.concatenate([one_row(m, second), one_row(m + 1, second)], axis=1)
-            y = jnp.dot(w, b, preferred_element_type=F32)
-            ybuf[m] = y[:, :HC]
-            ybuf[m + 1] = y[:, HC:]
-            return carry
-
         def one_edge(t):
             x = es[layer, t]
             return jnp.concatenate([pltpu.roll(x, d, 1), x, pltpu.roll(x, HC - d, 1)], axis=0)
 
-        def two_edges(i, carry):
-            t = lo + 2 * i
-            b = jnp.concatenate([one_edge(t), one_edge(t + 1)], axis=1)
-            y = jnp.dot(w, b, preferred_element_type=F32)
-            ye[t] = y[:, :HC]
-            ye[t + 1] = y[:, HC:]
-            return carry
-
-        count = (SPLIT - lo) // 2
-        lax.fori_loop(0, count, functools.partial(two_rows, lo, False), 0, unroll=count)
-        lax.fori_loop(0, count, functools.partial(two_rows, SPLIT, True), 0, unroll=count)
-        if layer < LAYERS - 1:
-            lax.fori_loop(0, (TILES - 2 * lo) // 2, two_edges, 0, unroll=(TILES - 2 * lo) // 2)
-        new = lo + HALO
-
-        def total(buf, m):
-            return buf[m - d, 0:64, :] + buf[m, 64:128, :] + buf[m + d, 128:192, :]
-
-        def finish(m, carry):
-            v = xs[layer, m].astype(F32) + jax.nn.gelu(total(ybuf, m))
+        def pair(one, buf, m):
+            y = jnp.dot(w, jnp.concatenate([one(m), one(m + 1)], axis=1), preferred_element_type=F32)
+            buf[m] = y[:, :HC]
+            buf[m + 1] = y[:, HC:]
+
+        def rows(first, last, second):
+            count = (last - first) // 2
+            loop(0, count, lambda i: pair(lambda m: one_row(m, second), y_of, first + 2 * i), count)
+
+        def edges(first, last):
+            count = (last - first) // 2
+            loop(0, count, lambda i: pair(one_edge, ye, first + 2 * i), count)
+
+        def finish(m):
+            v = xs[layer, m].astype(F32) + jax.nn.gelu(total(y_of, m, d))
             if layer < LAYERS - 1:
                 v = v * jnp.where(m < REACH, up_ok, jnp.where(m >= REACH + HR, down_ok, 1.0))
                 xs[layer + 1, m] = v.astype(BF)
             else:
                 fbuf[pl.ds(pl.multiple_of((m - REACH) * CHANNELS, CHANNELS), CHANNELS), :] = v
-            return carry
-
-        def finish_edge(t, carry):
-            v = (es[layer, t].astype(F32) + jax.nn.gelu(total(ye, t))) * edge_mask(t)
+
+        def finish_edge(t):
+            v = (es[layer, t].astype(F32) + jax.nn.gelu(total(ye, t, d))) * edge_mask(t)
             es[layer + 1, t] = v.astype(BF)
-            return carry
-
-        lax.fori_loop(new, ROWS - new, finish, 0, unroll=8)
-        if layer < LAYERS - 1:
-            lax.fori_loop(new, TILES - new, finish_edge, 0, unroll=4)
+
+        def repair(second):
+            def row(m):
+                edge = es[layer + 1, m - OFF if second else m]
+                v = xs[layer + 1, m]
+                v = jnp.where(lane < 2 * HALO, pltpu.roll(edge, 48 if second else 112, 1), v)
+                v = jnp.where(lane >= HC - 2 * HALO, pltpu.roll(edge, 16 if second else 80, 1), v)
+                xs[layer + 1, m] = v
+            return row
+
+        return rows, edges, finish, finish_edge, repair
+
+    arrived = [xs.at[0, pl.ds(0, 16)], xs.at[0, pl.ds(0, 2 * REACH)]]
+    top, bottom = REACH, REACH + HR
+    rows0, edges0, finish0, finish_edge0, _ = layer_ops(0)
+    rows1, edges1, finish1, finish_edge1, repair = layer_ops(1)
+    rows0(top, bottom, None)
+    loop(top + HALO, bottom - HALO, finish0, 24)
+    rows1(top + HALO, bottom - HALO, None)
+    loop(top + 2 * HALO, bottom - 2 * HALO, finish1, 16)
+    pltpu.make_async_copy(arrived[1], arrived[1], rsem.at[1]).wait()
+
+    @pl.when(n == 0)
+    def _():
+        xs[0, pl.ds(0, REACH)] = jnp.zeros((REACH, CHANNELS, HC), BF)
+
+    @pl.when(n == NN - 1)
+    def _():
+        xs[0, pl.ds(REACH + HR, REACH)] = jnp.zeros((REACH, CHANNELS, HC), BF)
+
+    rows0(0, top, None)
+    rows0(bottom, ROWS, None)
+    loop(HALO, top + HALO, finish0, 12)
+    loop(bottom - HALO, ROWS - HALO, finish0, 12)
+    rows1(HALO, top + HALO, None)
+    rows1(bottom - HALO, ROWS - HALO, None)
+    loop(2 * HALO, top + 2 * HALO, finish1, 12)
+    loop(bottom - 2 * HALO, ROWS - 2 * HALO, finish1, 12)
+    pltpu.make_async_copy(arrived[0], arrived[0], rsem.at[0]).wait()
+    loop(0, TILES, assemble, 12)
+    edges0(0, TILES)
+    loop(HALO, TILES - HALO, finish_edge0, 14)
+    edges1(HALO, TILES - HALO)
+    loop(2 * HALO, TILES - 2 * HALO, finish_edge1, 10)
+    loop(2 * HALO, SPLIT, repair(False), 20)
+    loop(SPLIT, ROWS - 2 * HALO, repair(True), 20)
+    rows2, _, finish2, _, _ = layer_ops(2)
+    rows2(2 * HALO, SPLIT, False)
+    rows2(SPLIT, ROWS - 2 * HALO, True)
+    loop(REACH, REACH + HR, finish2, 16)
 
     for c in range(CHANNELS):
         out[c] = fbuf[pl.ds(c, HR, stride=CHANNELS), :].astype(BF)
-    pltpu.make_async_copy(arrived, arrived, ssem.at[0]).wait()
+    for k in range(2):
+        pltpu.make_async_copy(arrived[k], arrived[k], ssem.at[k]).wait()
 
 
 def kernel(pick_h, feed_h, rates_h, win_h, gates_h, w_h, proj_h, taps_h, out,
@@ -350,8 +387,9 @@
     def put(i, v):
         xs[0, i + REACH] = v
 
-    blend(share, grid, hot2, t1, t2, projq, put)
-    conv(rates, wall, out, xs, es, strips, halo, ybuf, ye, fbuf, ssem, rsem)
+    blend(share, grid, hot2, t1, t2, projq, put,
+          lambda g: send_halo(g, xs, strips, halo, ssem, rsem))
+    conv(rates, wall, out, xs, es, halo, ybuf, ye, fbuf, ssem, rsem)
     sent()
 
 
@@ -376,14 +414,14 @@
             pltpu.VMEM((LAYERS, TILES, CHANNELS, HC), BF),
             pltpu.VMEM((2, HR // 8, CHANNELS, HC), BF),
             pltpu.VMEM((2, 8, CHANNELS, HC), BF),
-            pltpu.VMEM((ROWS, 3 * CHANNELS, HC), F32),
+            pltpu.VMEM((2, ROWS, 3 * CHANNELS, HC), F32),
             pltpu.VMEM((TILES, 3 * CHANNELS, HC), F32),
             pltpu.VMEM((HR * CHANNELS, HC), F32),
             pltpu.SMEM((1, 2, ND), jnp.int32), pltpu.SMEM((1, PMAX), jnp.int32), pltpu.VMEM((1, PMAX), jnp.int32),
             pltpu.SMEM((LAYERS,), jnp.int32), pltpu.VMEM((1, PMAX), jnp.int32), pltpu.VMEM((1, PMAX), jnp.int32),
             pltpu.VMEM((CHANNELS, 64), BF), pltpu.VMEM((LAYERS, 9, CHANNELS, CHANNELS), BF),
             pltpu.SemaphoreType.DMA((8,)), pltpu.SemaphoreType.DMA((8,)),
-            pltpu.SemaphoreType.DMA((1,)), pltpu.SemaphoreType.DMA((1,)),
+            pltpu.SemaphoreType.DMA((2,)), pltpu.SemaphoreType.DMA((2,)),
             pltpu.SemaphoreType.DMA((9,)),
         ],
         compiler_params=pltpu.CompilerParams(

time: 45.8 us -> 42.6 us (0.930)
  Pallas kernels: 43.8 us -> 40.6 us
    pallas_call x1, Pallas kernels: 43.8 us -> 40.6 us  [per_device(): pl.pallas_call(kernel, out_shape=jax.ShapeDtypeStruct((CHANNELS, HR, HC),...]
where the time goes in v4:
time: 42.6 us; the launch traced here: 42.5 us
  Pallas kernels  40.6 us (95%)
  local copies, waits for them, and re-layouts  1.87 us (4%)
    pallas_call x1, Pallas kernels, per_device(): pl.pallas_call(kernel, out_shape=jax.ShapeDtypeStruct((CHANNELS, HR, HC),...  40.6 us
    unnamed x1, local copies, waits for them, and re-layouts  1.87 us

profile of v4, /device:TPU:1, one launch (start us, length us, event | category | flops | bytes accessed | tf_op | source)
XLA Modules:
  0.0 42.5 jit_solution(7391338608237660409)
XLA Ops:
  0.0 40.6 %radar.1 = bf16[64,32,128]{2,1,0:T(8,128)(2,1)} custom-call(s32[1,2,128]{2,1,0:T(2,128)} %bitcast.1, s32[1,256]{1,0:T(1,128)} %feed_h.1, s32[3]{0:T(128)} %rates_h.1, s32[1,256]{1,0:T(1,128)} %win_h.1, bf16[256,16,128]{2,1,0:T(8,128)(2,1)} %gates_h.1, bf16[256,128,128]{2,1,0:T(8,128)(2,1)} %w_h.1, bf16[64,64]{1,0:T(8,128)(2,1)} %proj_h.1, ...), custom_call_target="tpu_custom_call" | custom-call | tf_op jit(solution)/shard_map/radar/pallas_call | solution.py:399
  40.6 1.9 %copy.10 = bf16[64,32,128]{2,1,0:T(8,128)(2,1)} copy(bf16[64,32,128]{2,1,0:T(8,128)(2,1)} %radar.1) | data formatting | bytes 1048576

commit v5 on v4

--- a/solution.py
+++ b/solution.py
@@ -20,8 +20,9 @@
 BF, F32 = jnp.bfloat16, jnp.float32
 
 
-NCH = 8
-CH = PMAX // NCH
+CHUNKS = 4
+CI, CJ = NN // CHUNKS, NE // CHUNKS
+GROUP = CI * NE
 REACH = LAYERS * HALO
 ROWS = HR + 2 * REACH
 TILES, OFF, SPLIT = 36, 20, 28
@@ -38,7 +39,7 @@
     return n, e, up, down, left, right
 
 
-def exchange(pick, gates, s0, s1, m0, m1, rows, ssem, rsem, bar, meanwhile, arrived):
+def exchange(pick, gates, s0, s1, m0, m1, rows, ssem, rsem, bar, gathered, meanwhile, arrived):
     n, e, up, down, left, right = places()
     f0, f1 = rows.at[0], rows.at[1]
 
@@ -55,7 +56,8 @@
                 s1[i, j] = v
         return carry
 
-    lax.fori_loop(0, ND, gather, 0, unroll=16)
+    lax.fori_loop(0, ND, gather, 0, unroll=64)
+    gathered()
     pl.semaphore_wait(bar, NE + NN - 2 + 4)
 
     def remote(src, dst, k, i, j):
@@ -64,12 +66,12 @@
             device_id=(lax.rem(n + i, NN), lax.rem(e + j, NE)), device_id_type=MESH,
         ).start()
 
-    for c in range(2):
-        for j in range(max(1, 8 * c), 8 * c + 8):
+    for c in range(CHUNKS):
+        for j in range(max(1, CJ * c), CJ * c + CJ):
             remote(s0.at[j], m0.at[j], c, 0, j)
             i = j // 2
             if j % 2 == 0 and i > 0:
-                remote(s1.at[i], m1.at[i], 2 + c, i, 0)
+                remote(s1.at[i], m1.at[i], CHUNKS + c, i, 0)
     m0[0] = s0[0]
     m1[0] = s1[0]
     meanwhile()
@@ -78,24 +80,26 @@
         r = rows.at[0, pl.ds(0, count)]
         pltpu.make_async_copy(r, r, sem).wait()
 
-    a_counts = (7 * NN, 8 * NN, 3 * NE, 4 * NE)
-    b_counts = (7 * 8, 7 * 8, 15 * 4, 15 * 4)
-    for c in range(2):
-        wait(a_counts[2 + c], rsem.at[2 + c])
+    a_counts = [(CJ - (c == 0)) * NN for c in range(CHUNKS)] + [(CI - (c == 0)) * NE for c in range(CHUNKS)]
+    b_counts = [(NN - 1) * CJ] * CHUNKS + [(NE - 1) * CI] * CHUNKS
+    counts = a_counts + b_counts
+    for c in range(CHUNKS):
+        wait(counts[CHUNKS + c], rsem.at[CHUNKS + c])
         for j in range(1, NE):
-            remote(m1.at[pl.ds(4 * c, 4), j], f1.at[pl.ds(j * NN + 4 * c, 4)], 6 + c, 0, j)
-        f1[pl.ds(4 * c, 4)] = m1[pl.ds(4 * c, 4), 0]
-        wait(a_counts[c], rsem.at[c])
+            remote(m1.at[pl.ds(CI * c, CI), j], f1.at[pl.ds(j * NN + CI * c, CI)], 3 * CHUNKS + c, 0, j)
+        f1[pl.ds(CI * c, CI)] = m1[pl.ds(CI * c, CI), 0]
+        wait(counts[c], rsem.at[c])
         for i in range(1, NN):
-            remote(m0.at[pl.ds(8 * c, 8), i], f0.at[pl.ds(i * NE + 8 * c, 8)], 4 + c, i, 0)
-        f0[pl.ds(8 * c, 8)] = m0[pl.ds(8 * c, 8), 0]
-    for c in range(2):
+            remote(m0.at[pl.ds(CJ * c, CJ), i], f0.at[pl.ds(i * NE + CJ * c, CJ)], 2 * CHUNKS + c, i, 0)
+        f0[pl.ds(CJ * c, CJ)] = m0[pl.ds(CJ * c, CJ), 0]
+    for c in range(CHUNKS):
         for k in (1, 0):
-            wait(b_counts[2 * k + c], rsem.at[4 + 2 * k + c])
+            at = (2 + k) * CHUNKS + c
+            wait(counts[at], rsem.at[at])
             arrived(k, c)
 
     def sent():
-        for k, count in enumerate(a_counts + b_counts):
+        for k, count in enumerate(counts):
             wait(count, ssem.at[k])
 
     return sent
@@ -106,7 +110,9 @@
     feed = feed_v[...]
     s, k = feed // 2, feed % 2
     i, j = (n + NN - s // NE) % NN, (e + NE - s % NE) % NE
-    q = jnp.where(feed < 0, -1, jnp.where(k == 0, i * NE + j, ND + j * NN + i))
+    q0 = j // CJ * 2 * GROUP + i * CJ + j % CJ
+    q1 = i // CI * 2 * GROUP + GROUP + j * CI + i % CI
+    q = jnp.where(feed < 0, -1, jnp.where(k == 0, q0, q1))
     down_q = jnp.transpose(jnp.broadcast_to(q, (128, PMAX)))
     number = iota((PMAX, 128), 0)
     uses = []
@@ -116,7 +122,7 @@
         uses.append(jnp.where(same, 1.0, 0.0).astype(BF))
     hot = jnp.where(win_v[...] == iota((GATES, PMAX), 0), 1.0, 0.0).astype(BF)
     hot = jnp.dot(hot, jnp.concatenate(uses, axis=1), preferred_element_type=F32).astype(BF)
-    hot2[...] = jnp.concatenate([hot, hot], axis=1)
+    hot2[...] = jnp.concatenate([hot[:, :128], hot[:, :128], hot[:, 128:], hot[:, 128:]], axis=1)
     col = iota((1, 512), 1)
     i1, w1, a1, b1, j1 = col // 128, col // 32 % 4, col // 16 % 2, col // 8 % 2, col % 8
     src1 = w1 * 128 + i1 * 32 + a1 * 16 + j1 * 2 + b1
@@ -133,29 +139,37 @@
             wall[layer, a * CHANNELS:(a + 1) * CHANNELS, :] = jnp.concatenate(line, axis=1).astype(BF)
 
 
-def products(k, c, entry, rows, wbuf, share):
+def products(k, c, entry, rows, wbuf, share, grid, hot2):
+    first = (2 * c + k) * GROUP
+
     def product(t, carry):
-        q = t // 8 * NE + 8 * c + lax.rem(t, 8) if k == 0 else t // 4 * NN + 4 * c + lax.rem(t, 4)
-        at = pl.multiple_of((k * ND + q) * FEATS, FEATS)
+        if k == 0:
+            q = t // CJ * NE + CJ * c + lax.rem(t, CJ)
+        else:
+            q = t // CI * NN + CI * c + lax.rem(t, CI)
+        at = pl.multiple_of((first + t) * FEATS, FEATS)
         share[pl.ds(at, FEATS), :] = jnp.dot(
-            rows[k, q], wbuf[entry[0, k * ND + q]], preferred_element_type=F32)
+            rows[k, q], wbuf[entry[0, first + t]], preferred_element_type=F32)
         return carry
 
-    lax.fori_loop(0, 64, product, 0, unroll=64)
-
-
-def blend(share, grid, hot2, t1, t2, projq, put, send):
+    lax.fori_loop(0, GROUP, product, 0, unroll=GROUP)
+    half, last = divmod(c, CHUNKS // 2)
+    if k == 1 or last < CHUNKS // 2 - 1:
+        return
     for f in range(0, FEATS, 2):
         parts = []
         for g in (f, f + 1):
-            v = share[pl.ds(g, PMAX, stride=FEATS), :]
+            v = share[pl.ds(half * 128 * FEATS + g, 128, stride=FEATS), :]
             hi = v.astype(BF)
             lo = (v - hi.astype(F32)).astype(BF)
             parts.append(jnp.concatenate([hi, lo], axis=0))
-        r = jnp.dot(hot2[...], jnp.concatenate(parts, axis=1), preferred_element_type=F32)
-        grid[pl.ds(f, 128, stride=FEATS), :] = r[:, :128]
-        grid[pl.ds(f + 1, 128, stride=FEATS), :] = r[:, 128:]
-
+        r = jnp.dot(hot2[:, half * 256:half * 256 + 256], jnp.concatenate(parts, axis=1), preferred_element_type=F32)
+        for g, v in ((f, r[:, :128]), (f + 1, r[:, 128:])):
+            at = pl.ds(g, 128, stride=FEATS)
+            grid[at, :] = v if half == 0 else grid[at, :] + v
+
+
+def blend(grid, t1, t2, projq, put, send):
     tiles = []
     for wh in range(4):
         line = []
@@ -214,7 +228,7 @@
         remote(xs.at[0, pl.ds(HR, REACH)], xs.at[0, pl.ds(0, REACH)], (down, e), 1)
 
 
-def conv(rates, wall, out, xs, es, halo, ybuf, ye, fbuf, ssem, rsem):
+def conv(rates, wall, out, xs, es, halo, ybuf, ye, ssem, rsem):
     n, e, up, down, left, right = places()
     lane = iota((CHANNELS, HC), 1)
     row_lane = iota((1, HC), 1)
@@ -290,7 +304,7 @@
                 v = v * jnp.where(m < REACH, up_ok, jnp.where(m >= REACH + HR, down_ok, 1.0))
                 xs[layer + 1, m] = v.astype(BF)
             else:
-                fbuf[pl.ds(pl.multiple_of((m - REACH) * CHANNELS, CHANNELS), CHANNELS), :] = v
+                out[m - REACH] = v.astype(BF)
 
         def finish_edge(t):
             v = (es[layer, t].astype(F32) + jax.nn.gelu(total(ye, t, d))) * edge_mask(t)
@@ -346,21 +360,19 @@
     rows2(SPLIT, ROWS - 2 * HALO, True)
     loop(REACH, REACH + HR, finish2, 16)
 
-    for c in range(CHANNELS):
-        out[c] = fbuf[pl.ds(c, HR, stride=CHANNELS), :].astype(BF)
     for k in range(2):
         pltpu.make_async_copy(arrived[k], arrived[k], ssem.at[k]).wait()
 
 
 def kernel(pick_h, feed_h, rates_h, win_h, gates_h, w_h, proj_h, taps_h, out,
            s0, s1, m0, m1, rows, gates, wbuf, share, grid, hot2, t1, t2, projq, wall,
-           xs, es, strips, halo, ybuf, ye, fbuf, pick, entry, entry_v, rates, feed_v, win_v, proj, taps,
+           xs, es, strips, halo, ybuf, ye, pick, entry, entry_v, rates, feed_v, win_v, proj, taps,
            asem, arem, ssem, rsem, lsem):
     n, e, up, down, left, right = places()
     pairs = [(pick_h, pick), (gates_h, gates), (rates_h, rates), (feed_h, feed_v), (win_h, win_v), (proj_h, proj), (taps_h, taps), (w_h, wbuf)]
     loads = [pltpu.make_async_copy(src, dst, lsem.at[k]) for k, (src, dst) in enumerate(pairs)]
-    for load in loads:
-        load.start()
+    loads[0].start()
+    loads[1].start()
     bar = pltpu.get_barrier_semaphore()
     for i in range(1, NE):
         pl.semaphore_signal(bar, inc=1, device_id=(n, lax.rem(e + i, NE)), device_id_type=MESH)
@@ -369,6 +381,8 @@
     for tn in (up, down):
         for te in (left, right):
             pl.semaphore_signal(bar, inc=1, device_id=(tn, te), device_id_type=MESH)
+    for load in loads[2:7]:
+        load.start()
     loads[0].wait()
     loads[1].wait()
 
@@ -381,15 +395,15 @@
         to_scalar.wait()
         loads[7].wait()
 
-    sent = exchange(pick, gates, s0, s1, m0, m1, rows, asem, arem, bar, meanwhile,
-                    lambda k, c: products(k, c, entry, rows, wbuf, share))
+    sent = exchange(pick, gates, s0, s1, m0, m1, rows, asem, arem, bar, loads[7].start, meanwhile,
+                    lambda k, c: products(k, c, entry, rows, wbuf, share, grid, hot2))
 
     def put(i, v):
         xs[0, i + REACH] = v
 
-    blend(share, grid, hot2, t1, t2, projq, put,
+    blend(grid, t1, t2, projq, put,
           lambda g: send_halo(g, xs, strips, halo, ssem, rsem))
-    conv(rates, wall, out, xs, es, halo, ybuf, ye, fbuf, ssem, rsem)
+    conv(rates, wall, out, xs, es, halo, ybuf, ye, ssem, rsem)
     sent()
 
 
@@ -398,7 +412,7 @@
     blk = (FEATS, GATES)
     return pl.pallas_call(
         kernel,
-        out_shape=jax.ShapeDtypeStruct((CHANNELS, HR, HC), BF),
+        out_shape=jax.ShapeDtypeStruct((HR, CHANNELS, HC), BF),
         in_specs=[hbm] * 8,
         out_specs=pl.BlockSpec(memory_space=pltpu.VMEM),
         scratch_shapes=[
@@ -416,18 +430,17 @@
             pltpu.VMEM((2, 8, CHANNELS, HC), BF),
             pltpu.VMEM((2, ROWS, 3 * CHANNELS, HC), F32),
             pltpu.VMEM((TILES, 3 * CHANNELS, HC), F32),
-            pltpu.VMEM((HR * CHANNELS, HC), F32),
             pltpu.SMEM((1, 2, ND), jnp.int32), pltpu.SMEM((1, PMAX), jnp.int32), pltpu.VMEM((1, PMAX), jnp.int32),
             pltpu.SMEM((LAYERS,), jnp.int32), pltpu.VMEM((1, PMAX), jnp.int32), pltpu.VMEM((1, PMAX), jnp.int32),
             pltpu.VMEM((CHANNELS, 64), BF), pltpu.VMEM((LAYERS, 9, CHANNELS, CHANNELS), BF),
-            pltpu.SemaphoreType.DMA((8,)), pltpu.SemaphoreType.DMA((8,)),
+            pltpu.SemaphoreType.DMA((4 * CHUNKS,)), pltpu.SemaphoreType.DMA((4 * CHUNKS,)),
             pltpu.SemaphoreType.DMA((2,)), pltpu.SemaphoreType.DMA((2,)),
             pltpu.SemaphoreType.DMA((9,)),
         ],
         compiler_params=pltpu.CompilerParams(
             collective_id=0, has_side_effects=True, vmem_limit_bytes=58 << 20),
         name="radar",
-    )(send_pick.transpose(0, 2, 1), feed, rates, window, gates, mixing_weight_blocks, proj_weight, conv_weight)
+    )(send_pick.transpose(0, 2, 1), feed, rates, window, gates, mixing_weight_blocks, proj_weight, conv_weight).transpose(1, 0, 2)
 
 
 def solution(mesh):

time: 42.6 us -> 41.7 us (0.979)
  Pallas kernels: 40.6 us -> 39.3 us
    transpose x0 -> x1, local copies, waits for them, and re-layouts: none -> 2.18 us  [per_device(): return pl.pallas_call(kernel, out_shape=jax.ShapeDtypeStruct((HR, CHANNEL...]
    unnamed x1 -> x0, local copies, waits for them, and re-layouts: 1.87 us -> none
    pallas_call x1, Pallas kernels: 40.6 us -> 39.3 us  [per_device(): pl.pallas_call(kernel, out_shape=jax.ShapeDtypeStruct((HR, CHANNELS, HC),...]
where the time goes in v5:
time: 41.7 us; the launch traced here: 41.5 us
  Pallas kernels  39.3 us (94%)
  local copies, waits for them, and re-layouts  2.18 us (5%)
    pallas_call x1, Pallas kernels, per_device(): pl.pallas_call(kernel, out_shape=jax.ShapeDtypeStruct((HR, CHANNELS, HC),...  39.3 us
    transpose x1, local copies, waits for them, and re-layouts, per_device(): return pl.pallas_call(kernel, out_shape=jax.ShapeDtypeStruct((HR, CHANNEL...  2.18 us

profile of v5, /device:TPU:1, one launch (start us, length us, event | category | flops | bytes accessed | tf_op | source)
XLA Modules:
  0.0 41.5 jit_solution(12537512831657184548)
XLA Ops:
  0.0 39.3 %radar.1 = bf16[32,64,128]{2,1,0:T(8,128)(2,1)} custom-call(s32[1,2,128]{2,1,0:T(2,128)} %bitcast.3, s32[1,256]{1,0:T(1,128)} %feed_h.1, s32[3]{0:T(128)} %rates_h.1, s32[1,256]{1,0:T(1,128)} %win_h.1, bf16[256,16,128]{2,1,0:T(8,128)(2,1)} %gates_h.1, bf16[256,128,128]{2,1,0:T(8,128)(2,1)} %w_h.1, bf16[64,64]{1,0:T(8,128)(2,1)} %proj_h.1, ...), custom_call_target="tpu_custom_call" | custom-call | tf_op jit(solution)/shard_map/radar/pallas_call | solution.py:413
  39.3 2.2 %copy.9 = bf16[64,32,128]{2,1,0:T(8,128)(2,1)} copy(bf16[64,32,128]{2,0,1:T(8,128)(2,1)} %bitcast.2) | data formatting | bytes 1048576 | tf_op jit(solution)/shard_map/transpose | solution.py:443

commit v6 on v5

--- a/solution.py
+++ b/solution.py
@@ -207,6 +207,10 @@
             src_ref=src, dst_ref=dst, send_sem=ssem.at[k], recv_sem=rsem.at[k],
             device_id=dev, device_id_type=MESH).start()
 
+    if g == 1:
+        remote(xs.at[0, pl.ds(REACH, REACH)], xs.at[0, pl.ds(REACH + HR, REACH)], (up, e), 1)
+    if g == 3:
+        remote(xs.at[0, pl.ds(HR, REACH)], xs.at[0, pl.ds(0, REACH)], (down, e), 1)
     sl = sr = jnp.zeros((CHANNELS, HC), BF)
     for k in range(8):
         v = xs[0, REACH + 8 * g + k]
@@ -222,10 +226,6 @@
             remote(own, halo.at[side, g - 2], (down, te))
         else:
             remote(own, halo.at[side, g + 6], (up, te))
-    if g == 1:
-        remote(xs.at[0, pl.ds(REACH, REACH)], xs.at[0, pl.ds(REACH + HR, REACH)], (up, e), 1)
-    if g == 3:
-        remote(xs.at[0, pl.ds(HR, REACH)], xs.at[0, pl.ds(0, REACH)], (down, e), 1)
 
 
 def conv(rates, wall, out, xs, es, halo, ybuf, ye, ssem, rsem):
@@ -348,17 +348,17 @@
     loop(2 * HALO, top + 2 * HALO, finish1, 12)
     loop(bottom - 2 * HALO, ROWS - 2 * HALO, finish1, 12)
     pltpu.make_async_copy(arrived[0], arrived[0], rsem.at[0]).wait()
-    loop(0, TILES, assemble, 12)
+    loop(0, TILES, assemble, 36)
     edges0(0, TILES)
-    loop(HALO, TILES - HALO, finish_edge0, 14)
+    loop(HALO, TILES - HALO, finish_edge0, 28)
     edges1(HALO, TILES - HALO)
-    loop(2 * HALO, TILES - 2 * HALO, finish_edge1, 10)
+    loop(2 * HALO, TILES - 2 * HALO, finish_edge1, 20)
     loop(2 * HALO, SPLIT, repair(False), 20)
     loop(SPLIT, ROWS - 2 * HALO, repair(True), 20)
     rows2, _, finish2, _, _ = layer_ops(2)
     rows2(2 * HALO, SPLIT, False)
     rows2(SPLIT, ROWS - 2 * HALO, True)
-    loop(REACH, REACH + HR, finish2, 16)
+    loop(REACH, REACH + HR, finish2, 32)
 
     for k in range(2):
         pltpu.make_async_copy(arrived[k], arrived[k], ssem.at[k]).wait()

time: 41.7 us -> 41.1 us (0.986)
  Pallas kernels: 39.3 us -> 38.7 us
    pallas_call x1, Pallas kernels: 39.3 us -> 38.7 us  [per_device(): pl.pallas_call(kernel, out_shape=jax.ShapeDtypeStruct((HR, CHANNELS, HC),...]
where the time goes in v6:
time: 41.1 us; the launch traced here: 40.9 us
  Pallas kernels  38.7 us (94%)
  local copies, waits for them, and re-layouts  2.18 us (5%)
    pallas_call x1, Pallas kernels, per_device(): pl.pallas_call(kernel, out_shape=jax.ShapeDtypeStruct((HR, CHANNELS, HC),...  38.7 us
    transpose x1, local copies, waits for them, and re-layouts, per_device(): return pl.pallas_call(kernel, out_shape=jax.ShapeDtypeStruct((HR, CHANNEL...  2.18 us

profile of v6, /device:TPU:1, one launch (start us, length us, event | category | flops | bytes accessed | tf_op | source)
XLA Modules:
  0.0 40.9 jit_solution(5685864541987256654)
XLA Ops:
  0.0 38.7 %radar.1 = bf16[32,64,128]{2,1,0:T(8,128)(2,1)} custom-call(s32[1,2,128]{2,1,0:T(2,128)} %bitcast.3, s32[1,256]{1,0:T(1,128)} %feed_h.1, s32[3]{0:T(128)} %rates_h.1, s32[1,256]{1,0:T(1,128)} %win_h.1, bf16[256,16,128]{2,1,0:T(8,128)(2,1)} %gates_h.1, bf16[256,128,128]{2,1,0:T(8,128)(2,1)} %w_h.1, bf16[64,64]{1,0:T(8,128)(2,1)} %proj_h.1, ...), custom_call_target="tpu_custom_call" | custom-call | tf_op jit(solution)/shard_map/radar/pallas_call | solution.py:413
  38.7 2.2 %copy.9 = bf16[64,32,128]{2,1,0:T(8,128)(2,1)} copy(bf16[64,32,128]{2,0,1:T(8,128)(2,1)} %bitcast.2) | data formatting | bytes 1048576 | tf_op jit(solution)/shard_map/transpose | solution.py:443
